TPU v7x, 128 devices: a whole 4x4x4 slice. The times are simulated.
128 devices in a mesh: seq: 16 (over z, x), chan: 4 (over y), dp: 2 (over core).
Axes of the slice: x: 4, y: 4, z: 4, core: 2. Of those that a mesh axis runs over, the one named last changes fastest.
Arguments:
- mr_query: bfloat16 [2, 8192, 2048], P('dp', 'chan', 'seq'), may hold values from -6 to 6
- mr_key: bfloat16 [2, 8192, 2048], P('dp', 'chan', 'seq'), may hold values from -6 to 6
- mr_value: bfloat16 [2, 8192, 2048], P('dp', 'chan', 'seq'), may hold values from -6 to 6
- li_key: bfloat16 [2, 8192, 2048], P('dp', 'chan', 'seq'), may hold values from -6 to 6
- li_value: bfloat16 [2, 8192, 2048], P('dp', 'chan', 'seq'), may hold values from -6 to 6
- grad_out: bfloat16 [2, 8192, 2048], P('dp', 'chan', 'seq'), may hold values from -6 to 6
- mr_filter: bfloat16 [512, 128], P('chan'), may hold values from -0.5 to 0.5
- li_residue: float32 [512, 16], P('chan'), may hold values from -1.5 to 1.5
- li_rate: float32 [512, 16], P('chan'), may hold values from 4.8828124e-06 to 0.05
Outputs:
- grad_mr_query: bfloat16 [2, 8192, 2048], P('dp', 'chan', 'seq')
- grad_mr_key: bfloat16 [2, 8192, 2048], P('dp', 'chan', 'seq')
- grad_mr_value: bfloat16 [2, 8192, 2048], P('dp', 'chan', 'seq')
- grad_li_key: bfloat16 [2, 8192, 2048], P('dp', 'chan', 'seq')
- grad_li_value: bfloat16 [2, 8192, 2048], P('dp', 'chan', 'seq')
- grad_filter: float32 [512, 128], P('chan')
- grad_residue: float32 [512, 16], P('chan')
All inputs are finite; a program needn't handle non-finite values.
Results may differ from a plain program's by a relative error of at most 0.012.
Values may be sent and summed in bfloat16 or wider, within the bound.
A program may use at most 128 MiB of HBM per device.

v0:
```python
import functools

import jax
import jax.numpy as jnp
from jax import lax
from jax.experimental import pallas as pl
from jax.experimental.pallas import tpu as pltpu
from jax.sharding import PartitionSpec as P

MESH = pl.DeviceIdType.MESH
NN = (((1,), (0,)), ((), ()))
NT = (((1,), (1,)), ((), ()))
EXACT = lax.Precision.HIGHEST
BF = jnp.bfloat16
F32 = jnp.float32

L = 128
C = 16
G = 8
X = 4
CHUNKS = 2


def dot(a, b, dims):
    return lax.dot_general(a, b, dims, preferred_element_type=F32)


def dot_exact(a, b, dims):
    return lax.dot_general(a, b, dims, precision=EXACT, preferred_element_type=F32)


def one_minus_exp_neg(x):
    acc = jnp.full_like(x, 1.0 / 40320.0)
    for divisor in (5040.0, 720.0, 120.0, 24.0, 6.0, 2.0, 1.0):
        acc = 1.0 / divisor - x * acc
    return x * acc


def kernel(
    nseq, q_h, k_h, v_h, lk_h, lv_h, go_h, filt, resid, rate,
    gq_h, gk_h, gv_h, glk_h, glv_h, gf_o, gr_o,
    q, k, v, lk, lv, go, gq, gk, gv, glk, glv,
    u1, u1p, dz2, dz1, dz1n, u2, du2, z2i,
    tp, tq, hs, tn, tv,
    r_s, coef_s, gain_s, s_loc, b_in, pref_b, pref_s,
    row_b, row_s, z_b, z_s, part, rs, dpx, total,
    in_sem, out_sem, halo_ss, halo_rs, halo2_ss, halo2_rs,
    xb_ss, xb_rs, zb_ss, zb_rs, xs_ss, xs_rs, zs_ss, zs_rs,
    rs_ss, rs_rs, dp_ss, dp_rs, ag_ss, ag_rs,
):
    channels = q.shape[0]
    nb = channels // L
    per = nb // CHUNKS
    Z = nseq // X
    me = lax.axis_index("seq")
    dp = lax.axis_index("dp")
    z = me // X
    x = me - z * X

    ins = ((q_h, q), (k_h, k), (go_h, go), (lv_h, lv), (lk_h, lk), (v_h, v))
    loads = [pltpu.make_async_copy(s, d, in_sem.at[i]) for i, (s, d) in enumerate(ins)]
    for load in loads:
        load.start()

    barrier = pltpu.get_barrier_semaphore()
    for d in range(1, nseq):
        pl.semaphore_signal(
            barrier, inc=1, device_id={"seq": lax.rem(me + d, nseq)}, device_id_type=MESH
        )
    pl.semaphore_signal(barrier, inc=1, device_id={"dp": 1 - dp}, device_id_type=MESH)

    def remote(src, dst, ss, rsem, **where):
        return pltpu.make_async_remote_copy(
            src_ref=src, dst_ref=dst, send_sem=ss, recv_sem=rsem,
            device_id=where, device_id_type=MESH,
        )

    sub = lax.broadcasted_iota(jnp.int32, (L, L), 0)
    lane = lax.broadcasted_iota(jnp.int32, (L, L), 1)
    sub_f = sub.astype(F32)
    same = (sub // C) == (lane // C)
    lower = lane >= sub
    rev = (sub + lane == L - 1).astype(F32).astype(BF)
    keep = sub + lane <= L - 1
    pick8 = lax.broadcasted_iota(jnp.int32, (G, L), 1) // C == lax.broadcasted_iota(
        jnp.int32, (G, L), 0
    )
    lane_group = lax.broadcasted_iota(jnp.int32, (1, L), 1) // C
    group_mask = [(lane_group == g).astype(F32).astype(BF) for g in range(G)]

    sel = (
        lax.broadcasted_iota(jnp.int32, (C, L), 1) % C
        == lax.broadcasted_iota(jnp.int32, (C, L), 0)
    ).astype(F32)
    spread = ((sub % G) == (lane // C))

    def to_rows(mat):
        wide = dot_exact(mat, sel, NN)
        return jnp.where(spread, wide, 0.0).reshape(nb, G, L).sum(axis=1)

    r_rows = to_rows(rate[...])
    gain_rows = jnp.sqrt(one_minus_exp_neg(2.0 * r_rows))
    r_s[...] = r_rows
    gain_s[...] = gain_rows
    coef_s[...] = to_rows(resid[...]) * gain_rows

    def rows(b):
        return pl.ds(pl.multiple_of(b * L, L), L)

    def tile(b):
        return pl.ds(pl.multiple_of(b * C, C), C)

    def blocks(ch, body):
        def step(i, carry):
            body(ch * per + i)
            return carry

        lax.fori_loop(0, per, step, 0)

    def big_rows(ch):
        return pl.ds(ch * per * L, per * L)

    def small_rows(ch):
        return pl.ds(ch * per * C, per * C)

    def f(ref, idx):
        return ref[idx, :].astype(F32)

    def squeeze_modes(full):
        return jnp.where(same, full, 0.0).reshape(G, C, L).sum(axis=0)

    def widen_modes(t):
        return jnp.where(same, jnp.concatenate([t] * G, axis=0), 0.0).astype(BF)

    def phase_a(ch):
        def body(b):
            u1[rows(b), :] = (f(q, rows(b)) * f(k, rows(b))).astype(BF)

        blocks(ch, body)

    def halo(ch):
        part_rows = big_rows(ch)
        return remote(
            u1.at[part_rows], u1p.at[part_rows], halo_ss.at[ch], halo_rs.at[ch],
            seq=lax.rem(me + 1, nseq),
        )

    def halo_back(ch):
        part_rows = big_rows(ch)
        return remote(
            dz1.at[part_rows], dz1n.at[part_rows], halo2_ss.at[ch], halo2_rs.at[ch],
            seq=lax.rem(me + nseq - 1, nseq),
        )

    def row_copy(ref, ss, rsem, ch, d):
        return remote(
            ref.at[x, small_rows(ch)], ref.at[x, small_rows(ch)], ss.at[ch, d], rsem.at[ch, d],
            seq=z * X + lax.rem(x + d, X),
        )

    def z_copy(ref, ss, rsem, ch, d, sign):
        to = lax.rem(z + sign * d + Z, Z)
        return remote(
            ref.at[z, small_rows(ch)], ref.at[z, small_rows(ch)], ss.at[ch, d], rsem.at[ch, d],
            seq=to * X + x,
        )

    def phase_b(ch):
        def body(b):
            d2 = (f(go, rows(b)) * f(lv, rows(b))).astype(BF)
            dz2[rows(b), :] = d2
            r = r_s[pl.ds(b, 1), :]
            powers = jnp.exp(-r * sub_f).astype(BF)
            tp[b] = powers
            tq[b] = jnp.exp(-r * (L - 1.0 - sub_f)).astype(BF)
            row_b[x, tile(b), :] = squeeze_modes(dot(d2, powers, NN)).astype(BF)

        blocks(ch, body)

    def phase_h(ch):
        def body(b):
            r = r_s[pl.ds(b, 1), :]
            powers = jnp.exp(-r * sub_f)
            amp = jnp.where(pick8, jnp.broadcast_to(coef_s[pl.ds(b, 1), :], (G, L)), 0.0)
            h = dot_exact(amp, powers, NT)
            d2 = dz2[rows(b), :]
            outs = []
            for g in range(G):
                circ = pltpu.roll(
                    jnp.broadcast_to(h[g : g + 1], (L, L)), 0, 1, stride=1, stride_axis=0
                )
                mat = jnp.where(lower, circ, 0.0).astype(BF)
                hs[b * G + g] = mat
                outs.append(dot(d2[g * C : (g + 1) * C], mat, NT))
            du2[rows(b), :] = jnp.concatenate(outs, axis=0)

        blocks(ch, body)

    def phase_t(ch):
        def body(b):
            fl = filt[pl.ds(pl.multiple_of(b * G, G), G), :]
            for g in range(G):
                circ = pltpu.roll(
                    jnp.broadcast_to(fl[g : g + 1], (L, L)), 0, 1, stride=1, stride_axis=0
                )
                tn[b * G + g] = jnp.where(lower, circ, 0.0).astype(BF)
                tv[b * G + g] = jnp.where(lower, 0.0, circ).astype(BF)

        blocks(ch, body)

    def decay(r, steps, ok):
        return jnp.where(ok, jnp.exp(-r * (L * jnp.maximum(steps, 0)).astype(F32)), 0.0)

    def mid(ch, row, pref, zref, back):
        def body(b):
            r = r_s[pl.ds(b, 1), :]
            before = jnp.zeros((C, L), F32)
            whole = jnp.zeros((C, L), F32)
            for src in range(X):
                val = row[src, tile(b), :].astype(F32)
                gap = (src - x - 1) if back else (x - 1 - src)
                before = before + decay(r, gap, gap >= 0) * val
                whole = whole + jnp.exp(-r * float(L * (src if back else X - 1 - src))) * val
            pref[tile(b), :] = before
            zref[z, tile(b), :] = whole.astype(BF)

        blocks(ch, body)

    def incoming(b, pref, zref, back):
        r = r_s[pl.ds(b, 1), :]
        acc = jnp.zeros((C, L), F32)
        for src in range(Z):
            gap = (src - z - 1) if back else (z - 1 - src)
            val = zref[src, tile(b), :].astype(F32)
            acc = acc + jnp.where(gap >= 0, decay(r, gap * X, gap >= 0) * val, 0.0)
        steps = (X - 1 - x) if back else x
        return pref[tile(b), :] + decay(r, steps, steps >= 0) * acc

    def scaled(b, state):
        r = r_s[pl.ds(b, 1), :]
        return widen_modes(coef_s[pl.ds(b, 1), :] * jnp.exp(-r) * state)

    def phase_bz(ch):
        def body(b):
            state = incoming(b, pref_b, z_b, True)
            b_in[tile(b), :] = state
            full = du2[rows(b), :] + dot(scaled(b, state), tq[b], NT)
            du2[rows(b), :] = full
            dz1[rows(b), :] = (full * f(lk, rows(b)) * f(v, rows(b))).astype(BF)

        blocks(ch, body)

    def phase_u(ch):
        def body(b):
            now, prev = u1[rows(b), :], u1p[rows(b), :]
            outs = []
            for g in range(G):
                part_g = slice(g * C, (g + 1) * C)
                outs.append(
                    dot(now[part_g], tn[b * G + g], NN) + dot(prev[part_g], tv[b * G + g], NN)
                )
            z1 = jnp.concatenate(outs, axis=0)
            y1 = (f(v, rows(b)) * z1).astype(BF).astype(F32)
            full = du2[rows(b), :]
            key = f(lk, rows(b))
            glk[rows(b), :] = (full * y1).astype(BF)
            gv[rows(b), :] = (full * key * z1).astype(BF)
            second = (y1 * key).astype(BF)
            u2[rows(b), :] = second
            state = squeeze_modes(dot(second, tq[b], NN))
            s_loc[tile(b), :] = state
            row_s[x, tile(b), :] = state.astype(BF)

        blocks(ch, body)

    def fold(mat):
        return pltpu.roll(mat, 1, 1, stride=1, stride_axis=0).sum(axis=0, keepdims=True)

    unfold = ((sub + lane) % L == 0).astype(F32)

    def phase_e(ch):
        def body(b):
            second = u2[rows(b), :]
            flip1 = dot(rev, dz1[rows(b), :], NT).astype(BF)
            flip2 = dot(rev, dz2[rows(b), :], NT).astype(BF)
            wide = jnp.concatenate([u1p[rows(b), :], u1[rows(b), :]], axis=1)
            lag1, lag2, outs = [], [], []
            for g in range(G):
                e1 = dot(flip1 * group_mask[g], wide, NN)
                lag1.append(fold(jnp.where(keep, e1[:, L:], e1[:, :L])))
                e2 = dot(flip2 * group_mask[g], second, NN)
                lag2.append(fold(jnp.where(keep, e2, 0.0)))
                outs.append(dot(second[g * C : (g + 1) * C], hs[b * G + g], NN))
            z2i[rows(b), :] = jnp.concatenate(outs, axis=0)
            filt_sum = dot_exact(jnp.concatenate(lag1, axis=0), unfold, NN)
            r = r_s[pl.ds(b, 1), :]
            table = jnp.exp(-r * ((L - sub) % L).astype(F32))
            inner = dot_exact(jnp.concatenate(lag2, axis=0), table, NN)
            inner = jnp.where(pick8, inner, 0.0).sum(axis=0, keepdims=True)
            cross = (s_loc[tile(b), :] * b_in[tile(b), :]).sum(axis=0, keepdims=True)
            res = gain_s[pl.ds(b, 1), :] * (inner + jnp.exp(-r) * cross)
            part[b, 0:G, :] = filt_sum
            part[b, G : 2 * G, :] = jnp.broadcast_to(res, (G, L))

        blocks(ch, body)

    def phase_sz(ch):
        def body(b):
            state = incoming(b, pref_s, z_s, False)
            full = z2i[rows(b), :] + dot(scaled(b, state), tp[b], NT)
            glv[rows(b), :] = (f(go, rows(b)) * full).astype(BF)

        blocks(ch, body)

    def phase_d(ch):
        def body(b):
            now, after = dz1[rows(b), :], dz1n[rows(b), :]
            outs = []
            for g in range(G):
                part_g = slice(g * C, (g + 1) * C)
                outs.append(
                    dot(now[part_g], tn[b * G + g], NT) + dot(after[part_g], tv[b * G + g], NT)
                )
            du1 = jnp.concatenate(outs, axis=0)
            gq[rows(b), :] = (du1 * f(k, rows(b))).astype(BF)
            gk[rows(b), :] = (du1 * f(q, rows(b))).astype(BF)

        blocks(ch, body)

    def start_row(ref, ss, rsem, ch):
        for d in range(1, X):
            row_copy(ref, ss, rsem, ch, d).start()

    def wait_row(ref, ss, rsem, ch):
        for d in range(1, X):
            row_copy(ref, ss, rsem, ch, d).wait_recv()

    def z_there(d, sign):
        return (z + d < Z) if sign > 0 else (z - d >= 0)

    def z_from(d, sign):
        return (z - d >= 0) if sign > 0 else (z + d < Z)

    def start_z(ref, ss, rsem, ch, sign):
        for d in range(1, Z):
            @pl.when(z_there(d, sign))
            def _():
                z_copy(ref, ss, rsem, ch, d, sign).start()

    def wait_z(ref, ss, rsem, ch, sign):
        for d in range(1, Z):
            @pl.when(z_from(d, sign))
            def _():
                z_copy(ref, ss, rsem, ch, d, sign).wait_recv()

    results = ((gq, gq_h), (gk, gk_h), (gv, gv_h), (glk, glk_h), (glv, glv_h))

    def save(i, ch):
        src, dst = results[i]
        part_rows = big_rows(ch)
        return pltpu.make_async_copy(src.at[part_rows], dst.at[part_rows], out_sem.at[i, ch])

    every = range(CHUNKS)

    @pl.when(me == 0)
    def _():
        u1p[...] = jnp.zeros_like(u1p)

    @pl.when(me == nseq - 1)
    def _():
        dz1n[...] = jnp.zeros_like(dz1n)

    loads[0].wait()
    loads[1].wait()
    for ch in every:
        phase_a(ch)
    pl.semaphore_wait(barrier, nseq)
    for ch in every:
        @pl.when(me < nseq - 1)
        def _():
            halo(ch).start()
    loads[2].wait()
    loads[3].wait()
    for ch in every:
        phase_b(ch)
        start_row(row_b, xb_ss, xb_rs, ch)
    for ch in every:
        phase_h(ch)
    for ch in every:
        wait_row(row_b, xb_ss, xb_rs, ch)
        mid(ch, row_b, pref_b, z_b, True)
        start_z(z_b, zb_ss, zb_rs, ch, -1)
    for ch in every:
        phase_t(ch)
    loads[4].wait()
    loads[5].wait()
    for ch in every:
        wait_z(z_b, zb_ss, zb_rs, ch, -1)
        phase_bz(ch)
        @pl.when(me > 0)
        def _():
            halo_back(ch).start()
    for ch in every:
        @pl.when(me > 0)
        def _():
            halo(ch).wait_recv()
        phase_u(ch)
        start_row(row_s, xs_ss, xs_rs, ch)
        save(2, ch).start()
        save(3, ch).start()
    for ch in every:
        phase_e(ch)
    for d in range(1, nseq):
        to = lax.rem(me + d, nseq)
        remote(part.at[to], rs.at[me], rs_ss.at[d], rs_rs.at[d], seq=to).start()
    for ch in every:
        wait_row(row_s, xs_ss, xs_rs, ch)
        mid(ch, row_s, pref_s, z_s, False)
        start_z(z_s, zs_ss, zs_rs, ch, 1)
    rs[me] = part[me]
    for d in range(1, nseq):
        to = lax.rem(me + d, nseq)
        remote(part.at[to], rs.at[me], rs_ss.at[d], rs_rs.at[d], seq=to).wait_recv()
    own = rs[0]
    for i in range(1, nseq):
        own = own + rs[i]
    dpx[0] = own
    swap = remote(dpx.at[0], dpx.at[1], dp_ss, dp_rs, dp=1 - dp)
    swap.start()
    for ch in every:
        wait_z(z_s, zs_ss, zs_rs, ch, 1)
        phase_sz(ch)
        save(4, ch).start()
    swap.wait_recv()
    total[me] = dpx[0] + dpx[1]
    for d in range(1, nseq):
        to = lax.rem(me + d, nseq)
        remote(total.at[me], total.at[me], ag_ss.at[d], ag_rs.at[d], seq=to).start()
    for ch in every:
        @pl.when(me < nseq - 1)
        def _():
            halo_back(ch).wait_recv()
        phase_d(ch)
        save(0, ch).start()
        save(1, ch).start()
    for d in range(1, nseq):
        to = lax.rem(me + d, nseq)
        remote(total.at[me], total.at[me], ag_ss.at[d], ag_rs.at[d], seq=to).wait_recv()
    final = total[...]
    gf_o[...] = final[:, :G, :].reshape(nb * G, L)
    gr_o[...] = dot_exact(
        jnp.where(spread, final[:, G:, :].reshape(nb * G, L), 0.0), sel, NT
    )

    for ch in every:
        @pl.when(me < nseq - 1)
        def _():
            halo(ch).wait_send()

        @pl.when(me > 0)
        def _():
            halo_back(ch).wait_send()

        for d in range(1, X):
            row_copy(row_b, xb_ss, xb_rs, ch, d).wait_send()
            row_copy(row_s, xs_ss, xs_rs, ch, d).wait_send()
        for d in range(1, Z):
            @pl.when(z_there(d, -1))
            def _():
                z_copy(z_b, zb_ss, zb_rs, ch, d, -1).wait_send()

            @pl.when(z_there(d, 1))
            def _():
                z_copy(z_s, zs_ss, zs_rs, ch, d, 1).wait_send()

        for i in range(5):
            save(i, ch).wait()
    swap.wait_send()
    for d in range(1, nseq):
        to = lax.rem(me + d, nseq)
        remote(part.at[to], rs.at[me], rs_ss.at[d], rs_rs.at[d], seq=to).wait_send()
        remote(total.at[me], total.at[me], ag_ss.at[d], ag_rs.at[d], seq=to).wait_send()


def per_device(nseq, q, k, v, lk, lv, go, filt, resid, rate):
    channels = q.shape[1]
    groups = filt.shape[0]
    nb = channels // L
    Z = nseq // X
    big = jax.ShapeDtypeStruct((channels, L), BF)
    hbm = pl.BlockSpec(memory_space=pl.ANY)
    vmem = pl.BlockSpec(memory_space=pltpu.VMEM)
    dma = pltpu.SemaphoreType.DMA
    bigs = [pltpu.VMEM((channels, L), BF)]
    outs = pl.pallas_call(
        functools.partial(kernel, nseq),
        out_shape=[big] * 5
        + [jax.ShapeDtypeStruct((groups, L), F32), jax.ShapeDtypeStruct((groups, C), F32)],
        in_specs=[hbm] * 6 + [vmem] * 3,
        out_specs=[hbm] * 5 + [vmem] * 2,
        scratch_shapes=bigs * 11
        + bigs * 6
        + [pltpu.VMEM((channels, L), F32)] * 2
        + [pltpu.VMEM((nb, L, L), BF)] * 2
        + [pltpu.VMEM((groups, L, L), BF)] * 3
        + [pltpu.VMEM((nb, L), F32)] * 3
        + [pltpu.VMEM((nb * C, L), F32)] * 4
        + [pltpu.VMEM((X, nb * C, L), BF)] * 2
        + [pltpu.VMEM((Z, nb * C, L), BF)] * 2
        + [pltpu.VMEM((nseq, 2 * G, L), F32)] * 2
        + [pltpu.VMEM((2, 2 * G, L), F32), pltpu.VMEM((nseq, 2 * G, L), F32)]
        + [dma((6,)), dma((5, CHUNKS))]
        + [dma((CHUNKS,))] * 4
        + [dma((CHUNKS, X))] * 2
        + [dma((CHUNKS, Z))] * 2
        + [dma((CHUNKS, X))] * 2
        + [dma((CHUNKS, Z))] * 2
        + [dma((nseq,))] * 2
        + [dma, dma]
        + [dma((nseq,))] * 2,
        compiler_params=pltpu.CompilerParams(
            collective_id=0, has_side_effects=True, vmem_limit_bytes=52 * 1024 * 1024
        ),
        name="hyena_bwd",
    )(
        q[0], k[0], v[0], lk[0], lv[0], go[0], filt.astype(F32), resid, rate
    )
    return tuple(o[None] for o in outs[:5]) + tuple(outs[5:])


def solution(mesh):
    wide = P("dp", "chan", "seq")
    small = P("chan", None)
    return jax.shard_map(
        functools.partial(per_device, mesh.shape["seq"]),
        mesh=mesh,
        in_specs=(wide,) * 6 + (small,) * 3,
        out_specs=(wide,) * 5 + (small,) * 2,
        check_vma=False,
    )
```

profile of v0, /device:TPU:1, one launch (start us, length us, event | category | flops | bytes accessed | tf_op | source)
XLA Modules:
  0.0 71.7 jit_solution(8564465835378008505)
XLA Ops:
  0.6 0.0 copy-start.2
  0.6 0.8 %convert_element_type.3.filt = f32[128,128]{1,0:T(8,128)S(1)} convert(bf16[128,128]{1,0:T(8,128)(2,1)} %param.15) | non-fusion elementwise | flops 16384 | bytes 98304 | tf_op jit(solution)/shard_map/convert_element_type | solution.py:526
  1.4 0.0 copy-done.2
  1.4 0.0 copy-start.3
  1.4 0.1 copy.16.resid
  1.5 0.6 copy-done.3
  2.1 0.1 copy.17.rate
  2.2 63.4 %hyena_bwd.1 = (bf16[2048,128]{1,0:T(8,128)(2,1)S(1)}, bf16[2048,128]{1,0:T(8,128)(2,1)S(1)}, bf16[2048,128]{1,0:T(8,128)(2,1)S(1)}, bf16[2048,128]{1,0:T(8,128)...) custom-call(bf16[2048,128]{1,0:T(8,128)(2,1)} %bitcast.14, ...), custom_call_target="tpu_custom_call" | custom-call | tf_op jit(solution)/shard_map/hyena_bwd/pallas_call | solution.py:495
  65.6 0.7 copy.18
  66.3 0.8 %copy.25 = bf16[1,2048,128]{2,1,0:T(8,128)(2,1)} copy(bf16[1,2048,128]{2,1,0:T(8,128)(2,1)S(1)} %bitcast.13) | data formatting | bytes 1048576
  67.1 0.8 %copy.26 = bf16[1,2048,128]{2,1,0:T(8,128)(2,1)} copy(bf16[1,2048,128]{2,1,0:T(8,128)(2,1)S(1)} %bitcast.12) | data formatting | bytes 1048576
  67.9 0.0 copy-start.1
  67.9 0.8 %copy.27 = bf16[1,2048,128]{2,1,0:T(8,128)(2,1)} copy(bf16[1,2048,128]{2,1,0:T(8,128)(2,1)S(1)} %bitcast.11) | data formatting | bytes 1048576
  68.6 0.4 copy-done.1
  69.1 0.0 copy-start
  69.1 0.8 %copy.28 = bf16[1,2048,128]{2,1,0:T(8,128)(2,1)} copy(bf16[1,2048,128]{2,1,0:T(8,128)(2,1)S(1)} %bitcast.21) | data formatting | bytes 1048576
  69.9 0.4 copy-done
  70.3 0.8 %copy.29 = bf16[1,2048,128]{2,1,0:T(8,128)(2,1)} copy(bf16[1,2048,128]{2,1,0:T(8,128)(2,1)S(1)} %bitcast.20) | data formatting | bytes 1048576
  71.1 0.6 copy.30
Async XLA Ops:
  0.6 0.8 %copy-start.2 = (f32[128,16]{0,1:T(8,128)S(1)}, f32[128,16]{0,1:T(8,128)}, u32[]{:S(2)}) copy-start(f32[128,16]{0,1:T(8,128)} %param.16) | copy-start | bytes 24580
  1.4 0.7 copy-start.3
  67.9 1.2 %copy-start.1 = (bf16[2048,128]{1,0:T(8,128)(2,1)S(1)}, bf16[2048,128]{1,0:T(8,128)(2,1)}, u32[]{:S(2)}) copy-start(bf16[2048,128]{1,0:T(8,128)(2,1)} %get-tuple-element.17) | copy-start | bytes 1572868
  69.1 1.2 %copy-start = (bf16[2048,128]{1,0:T(8,128)(2,1)S(1)}, bf16[2048,128]{1,0:T(8,128)(2,1)}, u32[]{:S(2)}) copy-start(bf16[2048,128]{1,0:T(8,128)(2,1)} %get-tuple-element.18) | copy-start | bytes 1572868
where the time goes:
time: 72.6 us; the launch traced here: 71.7 us
  Pallas kernels  63.4 us (87%)
  local copies, waits for them, and re-layouts  6.93 us (10%)
  other arithmetic  0.77 us (1%)
    pallas_call x1, Pallas kernels, per_device(): pl.pallas_call(functools.partial(kernel, nseq), out_shape=[big] * 5 + [ja...  63.4 us
    unnamed x17, local copies, waits for them, and re-layouts  6.93 us

commit v1 on v0

--- a/solution.py
+++ b/solution.py
@@ -10,6 +10,7 @@
 MESH = pl.DeviceIdType.MESH
 NN = (((1,), (0,)), ((), ()))
 NT = (((1,), (1,)), ((), ()))
+TN = (((0,), (0,)), ((), ()))
 EXACT = lax.Precision.HIGHEST
 BF = jnp.bfloat16
 F32 = jnp.float32
@@ -19,6 +20,8 @@
 G = 8
 X = 4
 CHUNKS = 2
+BATCH = 4
+WEIGHTS = 29
 
 
 def dot(a, b, dims):
@@ -41,8 +44,8 @@
     gq_h, gk_h, gv_h, glk_h, glv_h, gf_o, gr_o,
     q, k, v, lk, lv, go, gq, gk, gv, glk, glv,
     u1, u1p, dz2, dz1, dz1n, u2, du2, z2i,
-    tp, tq, hs, tn, tv,
-    r_s, coef_s, gain_s, s_loc, b_in, pref_b, pref_s,
+    tp, tq, hs, tw, h_s, f_s, lag1, lag2,
+    r_s, coef_s, gain_s, wt, s_loc, b_in, pref_b, pref_s,
     row_b, row_s, z_b, z_s, part, rs, dpx, total,
     in_sem, out_sem, halo_ss, halo_rs, halo2_ss, halo2_rs,
     xb_ss, xb_rs, zb_ss, zb_rs, xs_ss, xs_rs, zs_ss, zs_rs,
@@ -95,14 +98,35 @@
     spread = ((sub % G) == (lane // C))
 
     def to_rows(mat):
-        wide = dot_exact(mat, sel, NN)
+        wide = dot_exact(mat, sel, TN)
         return jnp.where(spread, wide, 0.0).reshape(nb, G, L).sum(axis=1)
 
     r_rows = to_rows(rate[...])
     gain_rows = jnp.sqrt(one_minus_exp_neg(2.0 * r_rows))
     r_s[...] = r_rows
     gain_s[...] = gain_rows
-    coef_s[...] = to_rows(resid[...]) * gain_rows
+    coef_rows = to_rows(resid[...]) * gain_rows
+    coef_s[...] = coef_rows
+    f_s[...] = filt[...].astype(F32)
+
+    def decay(steps):
+        if isinstance(steps, int):
+            return jnp.exp(-r_rows * float(L * steps))
+        ok = steps >= 0
+        return jnp.where(ok, jnp.exp(-r_rows * (L * jnp.maximum(steps, 0)).astype(F32)), 0.0)
+
+    for back in (0, 1):
+        base = back * 13
+        for i in range(X):
+            wt[base + i] = decay((i - x - 1) if back else (x - 1 - i))
+            wt[base + 4 + i] = decay(i if back else X - 1 - i)
+        for i in range(Z):
+            wt[base + 8 + i] = decay(X * ((i - z - 1) if back else (z - 1 - i)))
+        wt[base + 12] = decay((X - 1 - x) if back else x)
+    once = jnp.exp(-r_rows)
+    wt[26] = once
+    wt[27] = coef_rows * once
+    wt[28] = gain_rows
 
     def rows(b):
         return pl.ds(pl.multiple_of(b * L, L), L)
@@ -110,12 +134,22 @@
     def tile(b):
         return pl.ds(pl.multiple_of(b * C, C), C)
 
-    def blocks(ch, body):
+    def blocks(ch, body, batch=BATCH):
         def step(i, carry):
-            body(ch * per + i)
+            stores = []
+            for j in range(batch):
+                stores += body(ch * per + i * batch + j)
+            for ref, idx, value in stores:
+                ref[idx] = value
             return carry
 
-        lax.fori_loop(0, per, step, 0)
+        lax.fori_loop(0, per // batch, step, 0)
+
+    def row(ref, b):
+        return ref[pl.ds(b, 1), :]
+
+    def weight(i, b):
+        return wt[i, pl.ds(b, 1), :]
 
     def big_rows(ch):
         return pl.ds(ch * per * L, per * L)
@@ -133,10 +167,9 @@
         return jnp.where(same, jnp.concatenate([t] * G, axis=0), 0.0).astype(BF)
 
     def phase_a(ch):
-        def body(b):
-            u1[rows(b), :] = (f(q, rows(b)) * f(k, rows(b))).astype(BF)
-
-        blocks(ch, body)
+        blocks(ch, lambda b: [
+            (u1, rows(b), (f(q, rows(b)) * f(k, rows(b))).astype(BF))
+        ])
 
     def halo(ch):
         part_rows = big_rows(ch)
@@ -168,108 +201,121 @@
     def phase_b(ch):
         def body(b):
             d2 = (f(go, rows(b)) * f(lv, rows(b))).astype(BF)
-            dz2[rows(b), :] = d2
-            r = r_s[pl.ds(b, 1), :]
-            powers = jnp.exp(-r * sub_f).astype(BF)
-            tp[b] = powers
-            tq[b] = jnp.exp(-r * (L - 1.0 - sub_f)).astype(BF)
-            row_b[x, tile(b), :] = squeeze_modes(dot(d2, powers, NN)).astype(BF)
+            r = row(r_s, b)
+            powers = jnp.exp(-r * sub_f)
+            high = powers.astype(BF)
+            low = (powers - high.astype(F32)).astype(BF)
+            amp = jnp.where(pick8, jnp.broadcast_to(row(coef_s, b), (G, L)), 0.0)
+            amp_high = amp.astype(BF).astype(F32)
+            amps = jnp.concatenate([amp_high, amp - amp_high], axis=0).astype(BF)
+            h = dot(amps, high, NT) + dot(amps, low, NT)
+            state = squeeze_modes(dot(d2, high, NN))
+            return [
+                (dz2, rows(b), d2),
+                (tp, b, high),
+                (tq, b, jnp.exp(-r * (L - 1.0 - sub_f)).astype(BF)),
+                (h_s, octet(b), h[:G] + h[G:]),
+                (row_b, (x, tile(b)), state.astype(BF)),
+            ]
 
         blocks(ch, body)
 
+    def octet(b):
+        return pl.ds(pl.multiple_of(b * G, G), G)
+
+    def circulant(line):
+        return pltpu.roll(jnp.broadcast_to(line, (L, L)), 0, 1, stride=1, stride_axis=0)
+
     def phase_h(ch):
         def body(b):
-            r = r_s[pl.ds(b, 1), :]
-            powers = jnp.exp(-r * sub_f)
-            amp = jnp.where(pick8, jnp.broadcast_to(coef_s[pl.ds(b, 1), :], (G, L)), 0.0)
-            h = dot_exact(amp, powers, NT)
+            h = h_s[octet(b), :]
             d2 = dz2[rows(b), :]
-            outs = []
+            outs, stores = [], []
+            for g in range(0, G, 2):
+                mats = [
+                    jnp.where(lower, circulant(h[g + i : g + i + 1]), 0.0).astype(BF)
+                    for i in range(2)
+                ]
+                stores += [(hs, b * G + g + i, mats[i]) for i in range(2)]
+                pair = dot(d2[g * C : (g + 2) * C], jnp.concatenate(mats, axis=0), NT)
+                outs += [pair[:C, :L], pair[C:, L:]]
+            return stores + [(du2, rows(b), jnp.concatenate(outs, axis=0))]
+
+        blocks(ch, body, 2)
+
+    def phase_t(ch):
+        def body(b):
+            lines = f_s[octet(b), :]
+            stores = []
             for g in range(G):
-                circ = pltpu.roll(
-                    jnp.broadcast_to(h[g : g + 1], (L, L)), 0, 1, stride=1, stride_axis=0
+                circ = circulant(lines[g : g + 1])
+                mat = jnp.concatenate(
+                    [jnp.where(lower, 0.0, circ), jnp.where(lower, circ, 0.0)], axis=0
                 )
-                mat = jnp.where(lower, circ, 0.0).astype(BF)
-                hs[b * G + g] = mat
-                outs.append(dot(d2[g * C : (g + 1) * C], mat, NT))
-            du2[rows(b), :] = jnp.concatenate(outs, axis=0)
-
-        blocks(ch, body)
-
-    def phase_t(ch):
-        def body(b):
-            fl = filt[pl.ds(pl.multiple_of(b * G, G), G), :]
-            for g in range(G):
-                circ = pltpu.roll(
-                    jnp.broadcast_to(fl[g : g + 1], (L, L)), 0, 1, stride=1, stride_axis=0
-                )
-                tn[b * G + g] = jnp.where(lower, circ, 0.0).astype(BF)
-                tv[b * G + g] = jnp.where(lower, 0.0, circ).astype(BF)
-
-        blocks(ch, body)
-
-    def decay(r, steps, ok):
-        return jnp.where(ok, jnp.exp(-r * (L * jnp.maximum(steps, 0)).astype(F32)), 0.0)
-
-    def mid(ch, row, pref, zref, back):
-        def body(b):
-            r = r_s[pl.ds(b, 1), :]
+                stores.append((tw, b * G + g, mat.astype(BF)))
+            return stores
+
+        blocks(ch, body, 2)
+
+    def mid(ch, rref, pref, zref, back):
+        base = 13 * back
+
+        def body(b):
             before = jnp.zeros((C, L), F32)
             whole = jnp.zeros((C, L), F32)
             for src in range(X):
-                val = row[src, tile(b), :].astype(F32)
-                gap = (src - x - 1) if back else (x - 1 - src)
-                before = before + decay(r, gap, gap >= 0) * val
-                whole = whole + jnp.exp(-r * float(L * (src if back else X - 1 - src))) * val
-            pref[tile(b), :] = before
-            zref[z, tile(b), :] = whole.astype(BF)
+                val = rref[src, tile(b), :].astype(F32)
+                before = before + weight(base + src, b) * val
+                whole = whole + weight(base + 4 + src, b) * val
+            return [(pref, tile(b), before), (zref, (z, tile(b)), whole.astype(BF))]
 
         blocks(ch, body)
 
     def incoming(b, pref, zref, back):
-        r = r_s[pl.ds(b, 1), :]
+        base = 13 * back
         acc = jnp.zeros((C, L), F32)
         for src in range(Z):
             gap = (src - z - 1) if back else (z - 1 - src)
             val = zref[src, tile(b), :].astype(F32)
-            acc = acc + jnp.where(gap >= 0, decay(r, gap * X, gap >= 0) * val, 0.0)
-        steps = (X - 1 - x) if back else x
-        return pref[tile(b), :] + decay(r, steps, steps >= 0) * acc
+            acc = acc + jnp.where(gap >= 0, weight(base + 8 + src, b) * val, 0.0)
+        return pref[tile(b), :] + weight(base + 12, b) * acc
 
     def scaled(b, state):
-        r = r_s[pl.ds(b, 1), :]
-        return widen_modes(coef_s[pl.ds(b, 1), :] * jnp.exp(-r) * state)
+        return widen_modes(weight(27, b) * state)
 
     def phase_bz(ch):
         def body(b):
-            state = incoming(b, pref_b, z_b, True)
-            b_in[tile(b), :] = state
+            state = incoming(b, pref_b, z_b, 1)
             full = du2[rows(b), :] + dot(scaled(b, state), tq[b], NT)
-            du2[rows(b), :] = full
-            dz1[rows(b), :] = (full * f(lk, rows(b)) * f(v, rows(b))).astype(BF)
+            return [
+                (b_in, tile(b), state),
+                (du2, rows(b), full),
+                (dz1, rows(b), (full * f(lk, rows(b)) * f(v, rows(b))).astype(BF)),
+            ]
 
         blocks(ch, body)
 
     def phase_u(ch):
         def body(b):
-            now, prev = u1[rows(b), :], u1p[rows(b), :]
+            wide = jnp.concatenate([u1p[rows(b), :], u1[rows(b), :]], axis=1)
             outs = []
-            for g in range(G):
-                part_g = slice(g * C, (g + 1) * C)
-                outs.append(
-                    dot(now[part_g], tn[b * G + g], NN) + dot(prev[part_g], tv[b * G + g], NN)
-                )
+            for g in range(0, G, 2):
+                mats = jnp.concatenate([tw[b * G + g], tw[b * G + g + 1]], axis=1)
+                pair = dot(wide[g * C : (g + 2) * C], mats, NN)
+                outs += [pair[:C, :L], pair[C:, L:]]
             z1 = jnp.concatenate(outs, axis=0)
             y1 = (f(v, rows(b)) * z1).astype(BF).astype(F32)
             full = du2[rows(b), :]
             key = f(lk, rows(b))
-            glk[rows(b), :] = (full * y1).astype(BF)
-            gv[rows(b), :] = (full * key * z1).astype(BF)
             second = (y1 * key).astype(BF)
-            u2[rows(b), :] = second
             state = squeeze_modes(dot(second, tq[b], NN))
-            s_loc[tile(b), :] = state
-            row_s[x, tile(b), :] = state.astype(BF)
+            return [
+                (glk, rows(b), (full * y1).astype(BF)),
+                (gv, rows(b), (full * key * z1).astype(BF)),
+                (u2, rows(b), second),
+                (s_loc, tile(b), state),
+                (row_s, (x, tile(b)), state.astype(BF)),
+            ]
 
         blocks(ch, body)
 
@@ -278,52 +324,107 @@
 
     unfold = ((sub + lane) % L == 0).astype(F32)
 
+    def masked(flip):
+        return jnp.concatenate([flip * group_mask[g] for g in range(G)], axis=0)
+
     def phase_e(ch):
         def body(b):
+            flip = dot(rev, dz1[rows(b), :], NT).astype(BF)
+            wide = jnp.concatenate([u1p[rows(b), :], u1[rows(b), :]], axis=1)
+            energy = dot(masked(flip), wide, NN)
+            sums = [
+                fold(jnp.where(keep, energy[g * L : (g + 1) * L, L:], energy[g * L : (g + 1) * L, :L]))
+                for g in range(G)
+            ]
+            return [(lag1, octet(b), jnp.concatenate(sums, axis=0))]
+
+        blocks(ch, body, 2)
+
+    def phase_r(ch):
+        def pair(i, carry):
+            two = [ch * per + 2 * i, ch * per + 2 * i + 1]
+            flips = [masked(dot(rev, dz2[rows(b), :], NT).astype(BF)) for b in two]
+            zero = jnp.zeros((L, L), BF)
+            seconds = [u2[rows(b), :] for b in two]
+            diag = jnp.concatenate(
+                [
+                    jnp.concatenate([seconds[0], zero], axis=1),
+                    jnp.concatenate([zero, seconds[1]], axis=1),
+                ],
+                axis=0,
+            )
+            energy = dot(jnp.concatenate(flips, axis=1), diag, NN)
+            for j, b in enumerate(two):
+                sums = [
+                    fold(jnp.where(keep, energy[g * L : (g + 1) * L, j * L : (j + 1) * L], 0.0))
+                    for g in range(G)
+                ]
+                lag2[octet(b), :] = jnp.concatenate(sums, axis=0)
+            return carry
+
+        lax.fori_loop(0, per // 2, pair, 0)
+
+    def phase_z(ch):
+        def body(b):
             second = u2[rows(b), :]
-            flip1 = dot(rev, dz1[rows(b), :], NT).astype(BF)
-            flip2 = dot(rev, dz2[rows(b), :], NT).astype(BF)
-            wide = jnp.concatenate([u1p[rows(b), :], u1[rows(b), :]], axis=1)
-            lag1, lag2, outs = [], [], []
-            for g in range(G):
-                e1 = dot(flip1 * group_mask[g], wide, NN)
-                lag1.append(fold(jnp.where(keep, e1[:, L:], e1[:, :L])))
-                e2 = dot(flip2 * group_mask[g], second, NN)
-                lag2.append(fold(jnp.where(keep, e2, 0.0)))
-                outs.append(dot(second[g * C : (g + 1) * C], hs[b * G + g], NN))
-            z2i[rows(b), :] = jnp.concatenate(outs, axis=0)
-            filt_sum = dot_exact(jnp.concatenate(lag1, axis=0), unfold, NN)
-            r = r_s[pl.ds(b, 1), :]
-            table = jnp.exp(-r * ((L - sub) % L).astype(F32))
-            inner = dot_exact(jnp.concatenate(lag2, axis=0), table, NN)
-            inner = jnp.where(pick8, inner, 0.0).sum(axis=0, keepdims=True)
-            cross = (s_loc[tile(b), :] * b_in[tile(b), :]).sum(axis=0, keepdims=True)
-            res = gain_s[pl.ds(b, 1), :] * (inner + jnp.exp(-r) * cross)
-            part[b, 0:G, :] = filt_sum
-            part[b, G : 2 * G, :] = jnp.broadcast_to(res, (G, L))
+            outs = []
+            for g in range(0, G, 2):
+                mats = jnp.concatenate([hs[b * G + g], hs[b * G + g + 1]], axis=1)
+                pair = dot(second[g * C : (g + 2) * C], mats, NN)
+                outs += [pair[:C, :L], pair[C:, L:]]
+            return [(z2i, rows(b), jnp.concatenate(outs, axis=0))]
 
         blocks(ch, body)
 
+    def phase_g():
+        filt_sum = dot_exact(lag1[...], unfold, NN)
+        part[:, 0:G, :] = filt_sum.reshape(nb, G, L)
+        first = lane[:G] == 0
+
+        def step(i, carry):
+            for j in range(BATCH):
+                b = i * BATCH + j
+                lags = lag2[octet(b), :]
+                rest = jnp.where(first, 0.0, lags)
+                high = rest.astype(BF).astype(F32)
+                both = jnp.concatenate([high, rest - high], axis=0).astype(BF)
+                inner = dot(both, tq[b], NN)
+                inner = weight(26, b) * (inner[:G] + inner[G:]) + lags[:, 0:1]
+                inner = jnp.where(pick8, inner, 0.0).sum(axis=0, keepdims=True)
+                cross = (s_loc[tile(b), :] * b_in[tile(b), :]).sum(axis=0, keepdims=True)
+                res = weight(28, b) * (inner + weight(26, b) * cross)
+                part[b, G : 2 * G, :] = jnp.broadcast_to(res, (G, L))
+            return carry
+
+        lax.fori_loop(0, nb // BATCH, step, 0)
+
     def phase_sz(ch):
         def body(b):
-            state = incoming(b, pref_s, z_s, False)
+            state = incoming(b, pref_s, z_s, 0)
             full = z2i[rows(b), :] + dot(scaled(b, state), tp[b], NT)
-            glv[rows(b), :] = (f(go, rows(b)) * full).astype(BF)
+            return [(glv, rows(b), (f(go, rows(b)) * full).astype(BF))]
 
         blocks(ch, body)
 
     def phase_d(ch):
         def body(b):
-            now, after = dz1[rows(b), :], dz1n[rows(b), :]
+            wide = jnp.concatenate([dz1n[rows(b), :], dz1[rows(b), :]], axis=1)
             outs = []
-            for g in range(G):
-                part_g = slice(g * C, (g + 1) * C)
-                outs.append(
-                    dot(now[part_g], tn[b * G + g], NT) + dot(after[part_g], tv[b * G + g], NT)
+            for g in range(0, G, 2):
+                mats = jnp.concatenate(
+                    [
+                        jnp.concatenate([tw[b * G + g + i, :L], tw[b * G + g + i, L:]], axis=1)
+                        for i in range(2)
+                    ],
+                    axis=0,
                 )
+                pair = dot(wide[g * C : (g + 2) * C], mats, NT)
+                outs += [pair[:C, :L], pair[C:, L:]]
             du1 = jnp.concatenate(outs, axis=0)
-            gq[rows(b), :] = (du1 * f(k, rows(b))).astype(BF)
-            gk[rows(b), :] = (du1 * f(q, rows(b))).astype(BF)
+            return [
+                (gq, rows(b), (du1 * f(k, rows(b))).astype(BF)),
+                (gk, rows(b), (du1 * f(q, rows(b))).astype(BF)),
+            ]
 
         blocks(ch, body)
 
@@ -388,7 +489,7 @@
         phase_h(ch)
     for ch in every:
         wait_row(row_b, xb_ss, xb_rs, ch)
-        mid(ch, row_b, pref_b, z_b, True)
+        mid(ch, row_b, pref_b, z_b, 1)
         start_z(z_b, zb_ss, zb_rs, ch, -1)
     for ch in every:
         phase_t(ch)
@@ -410,13 +511,17 @@
         save(3, ch).start()
     for ch in every:
         phase_e(ch)
+        phase_r(ch)
+    phase_g()
     for d in range(1, nseq):
         to = lax.rem(me + d, nseq)
         remote(part.at[to], rs.at[me], rs_ss.at[d], rs_rs.at[d], seq=to).start()
     for ch in every:
         wait_row(row_s, xs_ss, xs_rs, ch)
-        mid(ch, row_s, pref_s, z_s, False)
+        mid(ch, row_s, pref_s, z_s, 0)
         start_z(z_s, zs_ss, zs_rs, ch, 1)
+    for ch in every:
+        phase_z(ch)
     rs[me] = part[me]
     for d in range(1, nseq):
         to = lax.rem(me + d, nseq)
@@ -449,7 +554,7 @@
     final = total[...]
     gf_o[...] = final[:, :G, :].reshape(nb * G, L)
     gr_o[...] = dot_exact(
-        jnp.where(spread, final[:, G:, :].reshape(nb * G, L), 0.0), sel, NT
+        sel, jnp.where(spread, final[:, G:, :].reshape(nb * G, L), 0.0), NT
     )
 
     for ch in every:
@@ -480,6 +585,15 @@
         to = lax.rem(me + d, nseq)
         remote(part.at[to], rs.at[me], rs_ss.at[d], rs_rs.at[d], seq=to).wait_send()
         remote(total.at[me], total.at[me], ag_ss.at[d], ag_rs.at[d], seq=to).wait_send()
+
+
+def save_kernel(*refs):
+    sems = refs[14]
+    copies = [pltpu.make_async_copy(refs[i], refs[7 + i], sems.at[i]) for i in range(7)]
+    for copy in copies:
+        copy.start()
+    for copy in copies:
+        copy.wait()
 
 
 def per_device(nseq, q, k, v, lk, lv, go, filt, resid, rate):
@@ -495,15 +609,17 @@
     outs = pl.pallas_call(
         functools.partial(kernel, nseq),
         out_shape=[big] * 5
-        + [jax.ShapeDtypeStruct((groups, L), F32), jax.ShapeDtypeStruct((groups, C), F32)],
-        in_specs=[hbm] * 6 + [vmem] * 3,
+        + [jax.ShapeDtypeStruct((groups, L), F32), jax.ShapeDtypeStruct((C, groups), F32)],
+        in_specs=[pl.BlockSpec(memory_space=pltpu.HBM)] * 6 + [vmem] * 3,
         out_specs=[hbm] * 5 + [vmem] * 2,
         scratch_shapes=bigs * 11
         + bigs * 6
         + [pltpu.VMEM((channels, L), F32)] * 2
         + [pltpu.VMEM((nb, L, L), BF)] * 2
-        + [pltpu.VMEM((groups, L, L), BF)] * 3
+        + [pltpu.VMEM((groups, L, L), BF), pltpu.VMEM((groups, 2 * L, L), BF)]
+        + [pltpu.VMEM((groups, L), F32)] * 4
         + [pltpu.VMEM((nb, L), F32)] * 3
+        + [pltpu.VMEM((WEIGHTS, nb, L), F32)]
         + [pltpu.VMEM((nb * C, L), F32)] * 4
         + [pltpu.VMEM((X, nb * C, L), BF)] * 2
         + [pltpu.VMEM((Z, nb * C, L), BF)] * 2
@@ -519,13 +635,23 @@
         + [dma, dma]
         + [dma((nseq,))] * 2,
         compiler_params=pltpu.CompilerParams(
-            collective_id=0, has_side_effects=True, vmem_limit_bytes=52 * 1024 * 1024
+            collective_id=0, has_side_effects=True, vmem_limit_bytes=32 * 1024 * 1024
         ),
         name="hyena_bwd",
     )(
-        q[0], k[0], v[0], lk[0], lv[0], go[0], filt.astype(F32), resid, rate
+        *[pltpu.with_memory_space_constraint(a[0], pltpu.HBM) for a in (q, k, v, lk, lv, go)],
+        filt, resid.T, rate.T,
     )
-    return tuple(o[None] for o in outs[:5]) + tuple(outs[5:])
+    outs = pl.pallas_call(
+        save_kernel,
+        out_shape=[jax.ShapeDtypeStruct(o.shape, o.dtype) for o in outs],
+        in_specs=[vmem] * 7,
+        out_specs=[hbm] * 7,
+        scratch_shapes=[dma((7,))],
+        compiler_params=pltpu.CompilerParams(vmem_limit_bytes=16 * 1024 * 1024),
+        name="hyena_save",
+    )(*outs)
+    return tuple(o[None] for o in outs[:5]) + (outs[5], outs[6].T)
 
 
 def solution(mesh):

time: 72.6 us -> 58.3 us (0.80)
  Pallas kernels: 63.4 us -> 55.2 us
  local copies, waits for them, and re-layouts: 6.93 us -> 2.14 us
  other arithmetic: 0.77 us -> 0 us
    pallas_call x1, Pallas kernels: 63.4 us -> 53.6 us  [per_device(): pl.pallas_call(functools.partial(kernel, nseq), out_shape=[big] * 5 + [ja...]
    unnamed x17 -> x6, local copies, waits for them, and re-layouts: 6.93 us -> 2.14 us
    pallas_call x0 -> x1, Pallas kernels: none -> 1.56 us  [per_device(): pl.pallas_call(save_kernel, out_shape=[jax.ShapeDtypeStruct(o.shape, o.dt...]
    convert_element_type x1 -> x0, other arithmetic: 0.77 us -> none  [per_device(): filt.astype(F32)]
where the time goes in v1:
time: 58.3 us; the launch traced here: 58 us
  Pallas kernels  55.2 us (95%)
  local copies, waits for them, and re-layouts  2.14 us (4%)
  between operations  0.65 us (1%)
    pallas_call x1, Pallas kernels, per_device(): pl.pallas_call(functools.partial(kernel, nseq), out_shape=[big] * 5 + [ja...  53.6 us
    unnamed x6, local copies, waits for them, and re-layouts  2.14 us
    pallas_call x1, Pallas kernels, per_device(): pl.pallas_call(save_kernel, out_shape=[jax.ShapeDtypeStruct(o.shape, o.dt...  1.56 us

profile of v1, /device:TPU:1, one launch (start us, length us, event | category | flops | bytes accessed | tf_op | source)
XLA Modules:
  0.0 58.0 jit_solution(14422771333488489154)
XLA Ops:
  0.6 0.0 copy-start.1
  0.6 0.7 %copy-done.1 = f32[128,16]{0,1:T(8,128)S(1)} copy-done((f32[128,16]{0,1:T(8,128)S(1)}, f32[128,16]{0,1:T(8,128)}, u32[]{:S(2)}) %copy-start.1) | copy-done | bytes 8216
  1.3 0.0 copy-start
  1.3 0.8 %copy-done = bf16[128,128]{1,0:T(8,128)(2,1)S(1)} copy-done((bf16[128,128]{1,0:T(8,128)(2,1)S(1)}, bf16[128,128]{1,0:T(8,128)(2,1)}, u32[]{:S(2)}) %copy-start) | copy-done | bytes 32792
  2.1 0.0 copy-start.2
  2.1 0.7 %copy-done.2 = f32[128,16]{0,1:T(8,128)S(1)} copy-done((f32[128,16]{0,1:T(8,128)S(1)}, f32[128,16]{0,1:T(8,128)}, u32[]{:S(2)}) %copy-start.2) | copy-done | bytes 8216
  2.8 53.6 %hyena_bwd.1 = (bf16[2048,128]{1,0:T(8,128)(2,1)S(1)}, bf16[2048,128]{1,0:T(8,128)(2,1)S(1)}, bf16[2048,128]{1,0:T(8,128)(2,1)S(1)}, bf16[2048,128]{1,0:T(8,128)...) custom-call(bf16[2048,128]{1,0:T(8,128)(2,1)} %bitcast.16, ...), custom_call_target="tpu_custom_call" | custom-call | tf_op jit(solution)/shard_map/hyena_bwd/pallas_call | solution.py:609
  56.4 1.6 %hyena_save.1 = (bf16[2048,128]{1,0:T(8,128)(2,1)}, bf16[2048,128]{1,0:T(8,128)(2,1)}, bf16[2048,128]{1,0:T(8,128)(2,1)}, bf16[2048,128]{1,0:T(8,128)(2,1)}, bf1...) custom-call(bf16[2048,128]{1,0:T(8,128)(2,1)S(1)} %get-tuple-element.21.refs_0_, ...), custom_call_target="tpu_custom_call" | custom-call | tf_op jit(solution)/shard_map/hyena_save/pallas_call | solution.py:645
Async XLA Ops:
  0.6 0.7 %copy-start.1 = (f32[128,16]{0,1:T(8,128)S(1)}, f32[128,16]{0,1:T(8,128)}, u32[]{:S(2)}) copy-start(f32[128,16]{0,1:T(8,128)} %param.16) | copy-start | bytes 24580
  1.3 0.8 %copy-start = (bf16[128,128]{1,0:T(8,128)(2,1)S(1)}, bf16[128,128]{1,0:T(8,128)(2,1)}, u32[]{:S(2)}) copy-start(bf16[128,128]{1,0:T(8,128)(2,1)} %filt.1) | copy-start | bytes 98308
  2.1 0.7 %copy-start.2 = (f32[128,16]{0,1:T(8,128)S(1)}, f32[128,16]{0,1:T(8,128)}, u32[]{:S(2)}) copy-start(f32[128,16]{0,1:T(8,128)} %param.17) | copy-start | bytes 24580

commit v2 on v1

--- a/solution.py
+++ b/solution.py
@@ -20,8 +20,9 @@
 G = 8
 X = 4
 CHUNKS = 2
-BATCH = 4
-WEIGHTS = 29
+BATCH = 8
+PIECES = 2
+WEIGHTS = 20
 
 
 def dot(a, b, dims):
@@ -40,16 +41,16 @@
 
 
 def kernel(
-    nseq, q_h, k_h, v_h, lk_h, lv_h, go_h, filt, resid, rate,
+    nseq, q_h, k_h, v_h, lk_h, lv_h, go_h, filt_h, resid_h, rate_h,
     gq_h, gk_h, gv_h, glk_h, glv_h, gf_o, gr_o,
-    q, k, v, lk, lv, go, gq, gk, gv, glk, glv,
+    filt, resid, rate, q, k, v, lk, lv, go, gq, gk, gv, glk, glv,
     u1, u1p, dz2, dz1, dz1n, u2, du2, z2i,
     tp, tq, hs, tw, h_s, f_s, lag1, lag2,
-    r_s, coef_s, gain_s, wt, s_loc, b_in, pref_b, pref_s,
-    row_b, row_s, z_b, z_s, part, rs, dpx, total,
+    r_s, coef_s, gain_s, wt, s_loc, b_in, tc_b, tc_s,
+    row_b, row_s, z_b, z_s, part, rs, dpx, total, y1_s, z1_s, res, res_dp, res_all,
     in_sem, out_sem, halo_ss, halo_rs, halo2_ss, halo2_rs,
     xb_ss, xb_rs, zb_ss, zb_rs, xs_ss, xs_rs, zs_ss, zs_rs,
-    rs_ss, rs_rs, dp_ss, dp_rs, ag_ss, ag_rs,
+    rs_ss, rs_rs, dp_ss, dp_rs, ag_ss, ag_rs, rd_ss, rd_rs, ra_ss, ra_rs,
 ):
     channels = q.shape[0]
     nb = channels // L
@@ -60,7 +61,10 @@
     z = me // X
     x = me - z * X
 
-    ins = ((q_h, q), (k_h, k), (go_h, go), (lv_h, lv), (lk_h, lk), (v_h, v))
+    ins = (
+        (rate_h, rate), (resid_h, resid), (go_h, go), (lv_h, lv),
+        (q_h, q), (k_h, k), (filt_h, filt), (lk_h, lk), (v_h, v),
+    )
     loads = [pltpu.make_async_copy(s, d, in_sem.at[i]) for i, (s, d) in enumerate(ins)]
     for load in loads:
         load.start()
@@ -91,6 +95,8 @@
     lane_group = lax.broadcasted_iota(jnp.int32, (1, L), 1) // C
     group_mask = [(lane_group == g).astype(F32).astype(BF) for g in range(G)]
 
+    loads[0].wait()
+    loads[1].wait()
     sel = (
         lax.broadcasted_iota(jnp.int32, (C, L), 1) % C
         == lax.broadcasted_iota(jnp.int32, (C, L), 0)
@@ -107,7 +113,6 @@
     gain_s[...] = gain_rows
     coef_rows = to_rows(resid[...]) * gain_rows
     coef_s[...] = coef_rows
-    f_s[...] = filt[...].astype(F32)
 
     def decay(steps):
         if isinstance(steps, int):
@@ -116,17 +121,17 @@
         return jnp.where(ok, jnp.exp(-r_rows * (L * jnp.maximum(steps, 0)).astype(F32)), 0.0)
 
     for back in (0, 1):
-        base = back * 13
         for i in range(X):
-            wt[base + i] = decay((i - x - 1) if back else (x - 1 - i))
-            wt[base + 4 + i] = decay(i if back else X - 1 - i)
+            ahead = (i > x) if back else (i < x)
+            near = (i - x - 1) if back else (x - 1 - i)
+            wt[8 * back + i] = decay(jnp.where(ahead, near, near + X))
         for i in range(Z):
-            wt[base + 8 + i] = decay(X * ((i - z - 1) if back else (z - 1 - i)))
-        wt[base + 12] = decay((X - 1 - x) if back else x)
+            wt[8 * back + X + i] = decay(X * ((i - z - 1) if back else (z - 1 - i)))
     once = jnp.exp(-r_rows)
-    wt[26] = once
-    wt[27] = coef_rows * once
-    wt[28] = gain_rows
+    wt[16] = decay(X)
+    wt[17] = once
+    wt[18] = coef_rows * once
+    wt[19] = gain_rows
 
     def rows(b):
         return pl.ds(pl.multiple_of(b * L, L), L)
@@ -171,24 +176,29 @@
             (u1, rows(b), (f(q, rows(b)) * f(k, rows(b))).astype(BF))
         ])
 
-    def halo(ch):
-        part_rows = big_rows(ch)
+    def piece_rows(i):
+        return pl.ds(i * (per // PIECES) * L, (per // PIECES) * L)
+
+    def halo(i):
+        part_rows = piece_rows(i)
         return remote(
-            u1.at[part_rows], u1p.at[part_rows], halo_ss.at[ch], halo_rs.at[ch],
+            u1.at[part_rows], u1p.at[part_rows], halo_ss.at[i], halo_rs.at[i],
             seq=lax.rem(me + 1, nseq),
         )
 
-    def halo_back(ch):
-        part_rows = big_rows(ch)
+    def halo_back(i):
+        part_rows = piece_rows(i)
         return remote(
-            dz1.at[part_rows], dz1n.at[part_rows], halo2_ss.at[ch], halo2_rs.at[ch],
+            dz1.at[part_rows], dz1n.at[part_rows], halo2_ss.at[i], halo2_rs.at[i],
             seq=lax.rem(me + nseq - 1, nseq),
         )
 
-    def row_copy(ref, ss, rsem, ch, d):
+    def x_copy(both, ref, ss, rsem, ch, d, sign):
+        to = lax.rem(x + d, X)
+        inclusive = jnp.where((to > x) if sign > 0 else (to < x), 1, 0)
         return remote(
-            ref.at[x, small_rows(ch)], ref.at[x, small_rows(ch)], ss.at[ch, d], rsem.at[ch, d],
-            seq=z * X + lax.rem(x + d, X),
+            both.at[inclusive, small_rows(ch)], ref.at[x, small_rows(ch)],
+            ss.at[ch, d], rsem.at[ch, d], seq=z * X + to,
         )
 
     def z_copy(ref, ss, rsem, ch, d, sign):
@@ -215,7 +225,7 @@
                 (tp, b, high),
                 (tq, b, jnp.exp(-r * (L - 1.0 - sub_f)).astype(BF)),
                 (h_s, octet(b), h[:G] + h[G:]),
-                (row_b, (x, tile(b)), state.astype(BF)),
+                (z_b, (z, tile(b)), state.astype(BF)),
             ]
 
         blocks(ch, body)
@@ -241,7 +251,7 @@
                 outs += [pair[:C, :L], pair[C:, L:]]
             return stores + [(du2, rows(b), jnp.concatenate(outs, axis=0))]
 
-        blocks(ch, body, 2)
+        blocks(ch, body, 4)
 
     def phase_t(ch):
         def body(b):
@@ -255,42 +265,52 @@
                 stores.append((tw, b * G + g, mat.astype(BF)))
             return stores
 
-        blocks(ch, body, 2)
-
-    def mid(ch, rref, pref, zref, back):
-        base = 13 * back
-
-        def body(b):
-            before = jnp.zeros((C, L), F32)
-            whole = jnp.zeros((C, L), F32)
-            for src in range(X):
-                val = rref[src, tile(b), :].astype(F32)
-                before = before + weight(base + src, b) * val
-                whole = whole + weight(base + 4 + src, b) * val
-            return [(pref, tile(b), before), (zref, (z, tile(b)), whole.astype(BF))]
+        blocks(ch, body, 4)
+
+    def mid(ch, zref, both, rref, back):
+        def body(b):
+            acc = jnp.zeros((C, L), F32)
+            for src in range(Z):
+                gap = (src - z - 1) if back else (z - 1 - src)
+                val = zref[src, tile(b), :].astype(F32)
+                acc = acc + jnp.where(gap >= 0, weight(8 * back + X + src, b) * val, 0.0)
+            whole = zref[z, tile(b), :].astype(F32) + weight(16, b) * acc
+            acc = acc.astype(BF)
+            return [
+                (both, (0, tile(b)), acc),
+                (both, (1, tile(b)), whole.astype(BF)),
+                (rref, (x, tile(b)), acc),
+            ]
 
         blocks(ch, body)
 
-    def incoming(b, pref, zref, back):
-        base = 13 * back
+    def incoming(b, rref, back):
         acc = jnp.zeros((C, L), F32)
-        for src in range(Z):
-            gap = (src - z - 1) if back else (z - 1 - src)
-            val = zref[src, tile(b), :].astype(F32)
-            acc = acc + jnp.where(gap >= 0, weight(base + 8 + src, b) * val, 0.0)
-        return pref[tile(b), :] + weight(base + 12, b) * acc
+        for src in range(X):
+            acc = acc + weight(8 * back + src, b) * rref[src, tile(b), :].astype(F32)
+        return acc
 
     def scaled(b, state):
-        return widen_modes(weight(27, b) * state)
+        return widen_modes(weight(18, b) * state)
 
     def phase_bz(ch):
         def body(b):
-            state = incoming(b, pref_b, z_b, 1)
+            state = incoming(b, row_b, 1)
             full = du2[rows(b), :] + dot(scaled(b, state), tq[b], NT)
             return [
                 (b_in, tile(b), state),
                 (du2, rows(b), full),
                 (dz1, rows(b), (full * f(lk, rows(b)) * f(v, rows(b))).astype(BF)),
+            ]
+
+        blocks(ch, body)
+
+    def phase_k(ch):
+        def body(b):
+            full = du2[rows(b), :]
+            return [
+                (glk, rows(b), (full * f(y1_s, rows(b))).astype(BF)),
+                (gv, rows(b), (full * f(lk, rows(b)) * z1_s[rows(b), :]).astype(BF)),
             ]
 
         blocks(ch, body)
@@ -304,17 +324,15 @@
                 pair = dot(wide[g * C : (g + 2) * C], mats, NN)
                 outs += [pair[:C, :L], pair[C:, L:]]
             z1 = jnp.concatenate(outs, axis=0)
-            y1 = (f(v, rows(b)) * z1).astype(BF).astype(F32)
-            full = du2[rows(b), :]
-            key = f(lk, rows(b))
-            second = (y1 * key).astype(BF)
+            y1 = (f(v, rows(b)) * z1).astype(BF)
+            second = (y1.astype(F32) * f(lk, rows(b))).astype(BF)
             state = squeeze_modes(dot(second, tq[b], NN))
             return [
-                (glk, rows(b), (full * y1).astype(BF)),
-                (gv, rows(b), (full * key * z1).astype(BF)),
+                (y1_s, rows(b), y1),
+                (z1_s, rows(b), z1),
                 (u2, rows(b), second),
                 (s_loc, tile(b), state),
-                (row_s, (x, tile(b)), state.astype(BF)),
+                (z_s, (z, tile(b)), state.astype(BF)),
             ]
 
         blocks(ch, body)
@@ -338,7 +356,7 @@
             ]
             return [(lag1, octet(b), jnp.concatenate(sums, axis=0))]
 
-        blocks(ch, body, 2)
+        blocks(ch, body, 4)
 
     def phase_r(ch):
         def pair(i, carry):
@@ -362,7 +380,7 @@
                 lag2[octet(b), :] = jnp.concatenate(sums, axis=0)
             return carry
 
-        lax.fori_loop(0, per // 2, pair, 0)
+        lax.fori_loop(0, per // 2, pair, 0, unroll=2)
 
     def phase_z(ch):
         def body(b):
@@ -376,12 +394,14 @@
 
         blocks(ch, body)
 
-    def phase_g():
-        filt_sum = dot_exact(lag1[...], unfold, NN)
-        part[:, 0:G, :] = filt_sum.reshape(nb, G, L)
+    def phase_gf():
+        part[...] = dot_exact(lag1[...], unfold, NN).reshape(nb, G, L)
+
+    def phase_gr():
         first = lane[:G] == 0
 
         def step(i, carry):
+            values = []
             for j in range(BATCH):
                 b = i * BATCH + j
                 lags = lag2[octet(b), :]
@@ -389,18 +409,19 @@
                 high = rest.astype(BF).astype(F32)
                 both = jnp.concatenate([high, rest - high], axis=0).astype(BF)
                 inner = dot(both, tq[b], NN)
-                inner = weight(26, b) * (inner[:G] + inner[G:]) + lags[:, 0:1]
+                inner = weight(17, b) * (inner[:G] + inner[G:]) + lags[:, 0:1]
                 inner = jnp.where(pick8, inner, 0.0).sum(axis=0, keepdims=True)
                 cross = (s_loc[tile(b), :] * b_in[tile(b), :]).sum(axis=0, keepdims=True)
-                res = weight(28, b) * (inner + weight(26, b) * cross)
-                part[b, G : 2 * G, :] = jnp.broadcast_to(res, (G, L))
+                values.append(weight(19, b) * (inner + weight(17, b) * cross))
+            for j in range(BATCH):
+                res[pl.ds(i * BATCH + j, 1), :] = values[j]
             return carry
 
         lax.fori_loop(0, nb // BATCH, step, 0)
 
     def phase_sz(ch):
         def body(b):
-            state = incoming(b, pref_s, z_s, 0)
+            state = incoming(b, row_s, 0)
             full = z2i[rows(b), :] + dot(scaled(b, state), tp[b], NT)
             return [(glv, rows(b), (f(go, rows(b)) * full).astype(BF))]
 
@@ -428,13 +449,13 @@
 
         blocks(ch, body)
 
-    def start_row(ref, ss, rsem, ch):
+    def start_x(both, ref, ss, rsem, ch, sign):
         for d in range(1, X):
-            row_copy(ref, ss, rsem, ch, d).start()
-
-    def wait_row(ref, ss, rsem, ch):
+            x_copy(both, ref, ss, rsem, ch, d, sign).start()
+
+    def wait_x(both, ref, ss, rsem, ch, sign):
         for d in range(1, X):
-            row_copy(ref, ss, rsem, ch, d).wait_recv()
+            x_copy(both, ref, ss, rsem, ch, d, sign).wait_recv()
 
     def z_there(d, sign):
         return (z + d < Z) if sign > 0 else (z - d >= 0)
@@ -471,104 +492,166 @@
     def _():
         dz1n[...] = jnp.zeros_like(dz1n)
 
-    loads[0].wait()
-    loads[1].wait()
+    def peer(d):
+        return lax.rem(me + d, nseq)
+
+    def scatter(d):
+        return remote(part.at[peer(d)], rs.at[me], rs_ss.at[d], rs_rs.at[d], seq=peer(d))
+
+    def gather(d):
+        return remote(total.at[me], total.at[me], ag_ss.at[d], ag_rs.at[d], seq=peer(d))
+
+    def gather_res(d):
+        return remote(res_all.at[me], res_all.at[me], ra_ss.at[d], ra_rs.at[d], seq=peer(d))
+
+    swap = remote(dpx.at[0], dpx.at[1], dp_ss, dp_rs, dp=1 - dp)
+    swap_res = remote(res, res_dp, rd_ss, rd_rs, dp=1 - dp)
+    peers = range(1, nseq)
+
+    def send_halo(ch):
+        for i in range(ch * PIECES, (ch + 1) * PIECES):
+            @pl.when(me < nseq - 1)
+            def _():
+                halo(i).start()
+
+    def send_back(ch):
+        for i in range(ch * PIECES, (ch + 1) * PIECES):
+            @pl.when(me > 0)
+            def _():
+                halo_back(i).start()
+
+    def run_u(ch):
+        for i in range(ch * PIECES, (ch + 1) * PIECES):
+            @pl.when(me > 0)
+            def _():
+                halo(i).wait_recv()
+        phase_u(ch)
+        start_z(z_s, zs_ss, zs_rs, ch, 1)
+
+    def run_bz(ch):
+        wait_x(tc_b, row_b, xb_ss, xb_rs, ch, -1)
+        phase_bz(ch)
+        send_back(ch)
+
+    def run_mid_b(ch):
+        wait_z(z_b, zb_ss, zb_rs, ch, -1)
+        mid(ch, z_b, tc_b, row_b, 1)
+        start_x(tc_b, row_b, xb_ss, xb_rs, ch, -1)
+
+    def run_mid_s(ch):
+        wait_z(z_s, zs_ss, zs_rs, ch, 1)
+        mid(ch, z_s, tc_s, row_s, 0)
+        start_x(tc_s, row_s, xs_ss, xs_rs, ch, 1)
+
+    def run_d(ch):
+        for i in range(ch * PIECES, (ch + 1) * PIECES):
+            @pl.when(me < nseq - 1)
+            def _():
+                halo_back(i).wait_recv()
+        phase_d(ch)
+        save(0, ch).start()
+        save(1, ch).start()
+
+    def run_sz(ch):
+        wait_x(tc_s, row_s, xs_ss, xs_rs, ch, 1)
+        phase_sz(ch)
+        save(4, ch).start()
+
+    def run_k(ch):
+        phase_k(ch)
+        save(2, ch).start()
+        save(3, ch).start()
+
+    loads[2].wait()
+    loads[3].wait()
+    for ch in every:
+        phase_b(ch)
+    loads[4].wait()
+    loads[5].wait()
     for ch in every:
         phase_a(ch)
     pl.semaphore_wait(barrier, nseq)
     for ch in every:
-        @pl.when(me < nseq - 1)
-        def _():
-            halo(ch).start()
-    loads[2].wait()
-    loads[3].wait()
-    for ch in every:
-        phase_b(ch)
-        start_row(row_b, xb_ss, xb_rs, ch)
+        start_z(z_b, zb_ss, zb_rs, ch, -1)
+    send_halo(0)
+    loads[6].wait()
+    f_s[...] = filt[...].astype(F32)
     for ch in every:
         phase_h(ch)
-    for ch in every:
-        wait_row(row_b, xb_ss, xb_rs, ch)
-        mid(ch, row_b, pref_b, z_b, 1)
-        start_z(z_b, zb_ss, zb_rs, ch, -1)
-    for ch in every:
+    phase_t(0)
+    for ch in every:
+        run_mid_b(ch)
+    for ch in range(1, CHUNKS):
+        send_halo(ch)
+    for ch in range(1, CHUNKS):
         phase_t(ch)
-    loads[4].wait()
-    loads[5].wait()
-    for ch in every:
-        wait_z(z_b, zb_ss, zb_rs, ch, -1)
-        phase_bz(ch)
-        @pl.when(me > 0)
-        def _():
-            halo_back(ch).start()
-    for ch in every:
-        @pl.when(me > 0)
-        def _():
-            halo(ch).wait_recv()
-        phase_u(ch)
-        start_row(row_s, xs_ss, xs_rs, ch)
-        save(2, ch).start()
-        save(3, ch).start()
-    for ch in every:
+    loads[7].wait()
+    loads[8].wait()
+    run_u(0)
+    for ch in every:
+        run_bz(ch)
+    phase_e(0)
+    run_mid_s(0)
+    phase_r(0)
+    for ch in range(1, CHUNKS):
+        run_u(ch)
         phase_e(ch)
+    phase_gf()
+    for d in peers:
+        scatter(d).start()
+    for ch in range(1, CHUNKS):
+        run_mid_s(ch)
         phase_r(ch)
-    phase_g()
-    for d in range(1, nseq):
-        to = lax.rem(me + d, nseq)
-        remote(part.at[to], rs.at[me], rs_ss.at[d], rs_rs.at[d], seq=to).start()
-    for ch in every:
-        wait_row(row_s, xs_ss, xs_rs, ch)
-        mid(ch, row_s, pref_s, z_s, 0)
-        start_z(z_s, zs_ss, zs_rs, ch, 1)
-    for ch in every:
-        phase_z(ch)
+    phase_gr()
+    swap_res.start()
     rs[me] = part[me]
-    for d in range(1, nseq):
-        to = lax.rem(me + d, nseq)
-        remote(part.at[to], rs.at[me], rs_ss.at[d], rs_rs.at[d], seq=to).wait_recv()
+    for d in peers:
+        scatter(d).wait_recv()
     own = rs[0]
     for i in range(1, nseq):
         own = own + rs[i]
     dpx[0] = own
-    swap = remote(dpx.at[0], dpx.at[1], dp_ss, dp_rs, dp=1 - dp)
     swap.start()
     for ch in every:
-        wait_z(z_s, zs_ss, zs_rs, ch, 1)
-        phase_sz(ch)
-        save(4, ch).start()
+        run_k(ch)
+    swap_res.wait_recv()
+    res_all[me] = res[...] + res_dp[...]
+    for d in peers:
+        gather_res(d).start()
     swap.wait_recv()
     total[me] = dpx[0] + dpx[1]
-    for d in range(1, nseq):
-        to = lax.rem(me + d, nseq)
-        remote(total.at[me], total.at[me], ag_ss.at[d], ag_rs.at[d], seq=to).start()
-    for ch in every:
+    for d in peers:
+        gather(d).start()
+    for ch in every:
+        phase_z(ch)
+    for ch in every:
+        run_d(ch)
+    for ch in every:
+        run_sz(ch)
+    for d in peers:
+        gather(d).wait_recv()
+    gf_o[...] = total[...].reshape(nb * G, L)
+    for d in peers:
+        gather_res(d).wait_recv()
+    res_sum = res_all[0]
+    for i in range(1, nseq):
+        res_sum = res_sum + res_all[i]
+    wide = jnp.broadcast_to(res_sum[:, None, :], (nb, G, L)).reshape(nb * G, L)
+    gr_o[...] = dot_exact(sel, jnp.where(spread, wide, 0.0), NT)
+
+    for i in range(CHUNKS * PIECES):
         @pl.when(me < nseq - 1)
         def _():
-            halo_back(ch).wait_recv()
-        phase_d(ch)
-        save(0, ch).start()
-        save(1, ch).start()
-    for d in range(1, nseq):
-        to = lax.rem(me + d, nseq)
-        remote(total.at[me], total.at[me], ag_ss.at[d], ag_rs.at[d], seq=to).wait_recv()
-    final = total[...]
-    gf_o[...] = final[:, :G, :].reshape(nb * G, L)
-    gr_o[...] = dot_exact(
-        sel, jnp.where(spread, final[:, G:, :].reshape(nb * G, L), 0.0), NT
-    )
-
-    for ch in every:
-        @pl.when(me < nseq - 1)
-        def _():
-            halo(ch).wait_send()
+            halo(i).wait_send()
 
         @pl.when(me > 0)
         def _():
-            halo_back(ch).wait_send()
-
+            halo_back(i).wait_send()
+
+    for ch in every:
         for d in range(1, X):
-            row_copy(row_b, xb_ss, xb_rs, ch, d).wait_send()
-            row_copy(row_s, xs_ss, xs_rs, ch, d).wait_send()
+            x_copy(tc_b, row_b, xb_ss, xb_rs, ch, d, -1).wait_send()
+            x_copy(tc_s, row_s, xs_ss, xs_rs, ch, d, 1).wait_send()
         for d in range(1, Z):
             @pl.when(z_there(d, -1))
             def _():
@@ -581,10 +664,11 @@
         for i in range(5):
             save(i, ch).wait()
     swap.wait_send()
-    for d in range(1, nseq):
-        to = lax.rem(me + d, nseq)
-        remote(part.at[to], rs.at[me], rs_ss.at[d], rs_rs.at[d], seq=to).wait_send()
-        remote(total.at[me], total.at[me], ag_ss.at[d], ag_rs.at[d], seq=to).wait_send()
+    swap_res.wait_send()
+    for d in peers:
+        scatter(d).wait_send()
+        gather(d).wait_send()
+        gather_res(d).wait_send()
 
 
 def save_kernel(*refs):
@@ -610,9 +694,14 @@
         functools.partial(kernel, nseq),
         out_shape=[big] * 5
         + [jax.ShapeDtypeStruct((groups, L), F32), jax.ShapeDtypeStruct((C, groups), F32)],
-        in_specs=[pl.BlockSpec(memory_space=pltpu.HBM)] * 6 + [vmem] * 3,
+        in_specs=[pl.BlockSpec(memory_space=pltpu.HBM)] * 9,
         out_specs=[hbm] * 5 + [vmem] * 2,
-        scratch_shapes=bigs * 11
+        scratch_shapes=[
+            pltpu.VMEM((groups, L), BF),
+            pltpu.VMEM((C, groups), F32),
+            pltpu.VMEM((C, groups), F32),
+        ]
+        + bigs * 11
         + bigs * 6
         + [pltpu.VMEM((channels, L), F32)] * 2
         + [pltpu.VMEM((nb, L, L), BF)] * 2
@@ -620,17 +709,23 @@
         + [pltpu.VMEM((groups, L), F32)] * 4
         + [pltpu.VMEM((nb, L), F32)] * 3
         + [pltpu.VMEM((WEIGHTS, nb, L), F32)]
-        + [pltpu.VMEM((nb * C, L), F32)] * 4
+        + [pltpu.VMEM((nb * C, L), F32)] * 2
+        + [pltpu.VMEM((2, nb * C, L), BF)] * 2
         + [pltpu.VMEM((X, nb * C, L), BF)] * 2
         + [pltpu.VMEM((Z, nb * C, L), BF)] * 2
-        + [pltpu.VMEM((nseq, 2 * G, L), F32)] * 2
-        + [pltpu.VMEM((2, 2 * G, L), F32), pltpu.VMEM((nseq, 2 * G, L), F32)]
-        + [dma((6,)), dma((5, CHUNKS))]
-        + [dma((CHUNKS,))] * 4
+        + [pltpu.VMEM((nseq, G, L), F32)] * 2
+        + [pltpu.VMEM((2, G, L), F32), pltpu.VMEM((nseq, G, L), F32)]
+        + [pltpu.VMEM((channels, L), BF), pltpu.VMEM((channels, L), F32)]
+        + [pltpu.VMEM((nb, L), F32)] * 2
+        + [pltpu.VMEM((nseq, nb, L), F32)]
+        + [dma((9,)), dma((5, CHUNKS))]
+        + [dma((CHUNKS * PIECES,))] * 4
         + [dma((CHUNKS, X))] * 2
         + [dma((CHUNKS, Z))] * 2
         + [dma((CHUNKS, X))] * 2
         + [dma((CHUNKS, Z))] * 2
+        + [dma((nseq,))] * 2
+        + [dma, dma]
         + [dma((nseq,))] * 2
         + [dma, dma]
         + [dma((nseq,))] * 2,
@@ -639,8 +734,10 @@
         ),
         name="hyena_bwd",
     )(
-        *[pltpu.with_memory_space_constraint(a[0], pltpu.HBM) for a in (q, k, v, lk, lv, go)],
-        filt, resid.T, rate.T,
+        *[
+            pltpu.with_memory_space_constraint(a, pltpu.HBM)
+            for a in (q[0], k[0], v[0], lk[0], lv[0], go[0], filt, resid.T, rate.T)
+        ]
     )
     outs = pl.pallas_call(
         save_kernel,

time: 58.3 us -> 48.3 us (0.83)
  Pallas kernels: 55.2 us -> 47.5 us
  local copies, waits for them, and re-layouts: 2.14 us -> 0 us
    pallas_call x1, Pallas kernels: 53.6 us -> 46 us  [per_device(): pl.pallas_call(functools.partial(kernel, nseq), out_shape=[big] * 5 + [ja...]
    unnamed x6 -> x0, local copies, waits for them, and re-layouts: 2.14 us -> none
where the time goes in v2:
time: 48.3 us; the launch traced here: 48.2 us
  Pallas kernels  47.5 us (98%)
  between operations  0.64 us (1%)
    pallas_call x1, Pallas kernels, per_device(): pl.pallas_call(functools.partial(kernel, nseq), out_shape=[big] * 5 + [ja...  46 us
    pallas_call x1, Pallas kernels, per_device(): pl.pallas_call(save_kernel, out_shape=[jax.ShapeDtypeStruct(o.shape, o.dt...  1.56 us

profile of v2, /device:TPU:1, one launch (start us, length us, event | category | flops | bytes accessed | tf_op | source)
XLA Modules:
  0.0 48.2 jit_solution(9663267944022277418)
XLA Ops:
  0.6 46.0 %hyena_bwd.1 = (bf16[2048,128]{1,0:T(8,128)(2,1)S(1)}, bf16[2048,128]{1,0:T(8,128)(2,1)S(1)}, bf16[2048,128]{1,0:T(8,128)(2,1)S(1)}, bf16[2048,128]{1,0:T(8,128)...) custom-call(bf16[2048,128]{1,0:T(8,128)(2,1)} %bitcast.14, ...), custom_call_target="tpu_custom_call" | custom-call | tf_op jit(solution)/shard_map/hyena_bwd/pallas_call | solution.py:693
  46.6 1.6 %hyena_save.1 = (bf16[2048,128]{1,0:T(8,128)(2,1)}, bf16[2048,128]{1,0:T(8,128)(2,1)}, bf16[2048,128]{1,0:T(8,128)(2,1)}, bf16[2048,128]{1,0:T(8,128)(2,1)}, bf1...) custom-call(bf16[2048,128]{1,0:T(8,128)(2,1)S(1)} %get-tuple-element.21.refs_0_, ...), custom_call_target="tpu_custom_call" | custom-call | tf_op jit(solution)/shard_map/hyena_save/pallas_call | solution.py:742

commit v3 on v2

--- a/solution.py
+++ b/solution.py
@@ -62,8 +62,8 @@
     x = me - z * X
 
     ins = (
-        (rate_h, rate), (resid_h, resid), (go_h, go), (lv_h, lv),
-        (q_h, q), (k_h, k), (filt_h, filt), (lk_h, lk), (v_h, v),
+        (q_h, q), (k_h, k), (rate_h, rate), (resid_h, resid), (go_h, go),
+        (lv_h, lv), (filt_h, filt), (lk_h, lk), (v_h, v),
     )
     loads = [pltpu.make_async_copy(s, d, in_sem.at[i]) for i, (s, d) in enumerate(ins)]
     for load in loads:
@@ -94,44 +94,6 @@
     )
     lane_group = lax.broadcasted_iota(jnp.int32, (1, L), 1) // C
     group_mask = [(lane_group == g).astype(F32).astype(BF) for g in range(G)]
-
-    loads[0].wait()
-    loads[1].wait()
-    sel = (
-        lax.broadcasted_iota(jnp.int32, (C, L), 1) % C
-        == lax.broadcasted_iota(jnp.int32, (C, L), 0)
-    ).astype(F32)
-    spread = ((sub % G) == (lane // C))
-
-    def to_rows(mat):
-        wide = dot_exact(mat, sel, TN)
-        return jnp.where(spread, wide, 0.0).reshape(nb, G, L).sum(axis=1)
-
-    r_rows = to_rows(rate[...])
-    gain_rows = jnp.sqrt(one_minus_exp_neg(2.0 * r_rows))
-    r_s[...] = r_rows
-    gain_s[...] = gain_rows
-    coef_rows = to_rows(resid[...]) * gain_rows
-    coef_s[...] = coef_rows
-
-    def decay(steps):
-        if isinstance(steps, int):
-            return jnp.exp(-r_rows * float(L * steps))
-        ok = steps >= 0
-        return jnp.where(ok, jnp.exp(-r_rows * (L * jnp.maximum(steps, 0)).astype(F32)), 0.0)
-
-    for back in (0, 1):
-        for i in range(X):
-            ahead = (i > x) if back else (i < x)
-            near = (i - x - 1) if back else (x - 1 - i)
-            wt[8 * back + i] = decay(jnp.where(ahead, near, near + X))
-        for i in range(Z):
-            wt[8 * back + X + i] = decay(X * ((i - z - 1) if back else (z - 1 - i)))
-    once = jnp.exp(-r_rows)
-    wt[16] = decay(X)
-    wt[17] = once
-    wt[18] = coef_rows * once
-    wt[19] = gain_rows
 
     def rows(b):
         return pl.ds(pl.multiple_of(b * L, L), L)
@@ -508,14 +470,14 @@
     swap_res = remote(res, res_dp, rd_ss, rd_rs, dp=1 - dp)
     peers = range(1, nseq)
 
-    def send_halo(ch):
-        for i in range(ch * PIECES, (ch + 1) * PIECES):
+    def send_halo(*pieces):
+        for i in pieces:
             @pl.when(me < nseq - 1)
             def _():
                 halo(i).start()
 
-    def send_back(ch):
-        for i in range(ch * PIECES, (ch + 1) * PIECES):
+    def send_back(*pieces):
+        for i in pieces:
             @pl.when(me > 0)
             def _():
                 halo_back(i).start()
@@ -531,7 +493,6 @@
     def run_bz(ch):
         wait_x(tc_b, row_b, xb_ss, xb_rs, ch, -1)
         phase_bz(ch)
-        send_back(ch)
 
     def run_mid_b(ch):
         wait_z(z_b, zb_ss, zb_rs, ch, -1)
@@ -562,18 +523,55 @@
         save(2, ch).start()
         save(3, ch).start()
 
+    loads[0].wait()
+    loads[1].wait()
+    for ch in every:
+        phase_a(ch)
     loads[2].wait()
     loads[3].wait()
-    for ch in every:
-        phase_b(ch)
+    sel = (
+        lax.broadcasted_iota(jnp.int32, (C, L), 1) % C
+        == lax.broadcasted_iota(jnp.int32, (C, L), 0)
+    ).astype(F32)
+    spread = ((sub % G) == (lane // C))
+
+    def to_rows(mat):
+        wide = dot_exact(mat, sel, TN)
+        return jnp.where(spread, wide, 0.0).reshape(nb, G, L).sum(axis=1)
+
+    r_rows = to_rows(rate[...])
+    gain_rows = jnp.sqrt(one_minus_exp_neg(2.0 * r_rows))
+    r_s[...] = r_rows
+    gain_s[...] = gain_rows
+    coef_rows = to_rows(resid[...]) * gain_rows
+    coef_s[...] = coef_rows
+
+    def decay(steps):
+        if isinstance(steps, int):
+            return jnp.exp(-r_rows * float(L * steps))
+        ok = steps >= 0
+        return jnp.where(ok, jnp.exp(-r_rows * (L * jnp.maximum(steps, 0)).astype(F32)), 0.0)
+
+    for back in (0, 1):
+        for i in range(X):
+            ahead = (i > x) if back else (i < x)
+            near = (i - x - 1) if back else (x - 1 - i)
+            wt[8 * back + i] = decay(jnp.where(ahead, near, near + X))
+        for i in range(Z):
+            wt[8 * back + X + i] = decay(X * ((i - z - 1) if back else (z - 1 - i)))
+    once = jnp.exp(-r_rows)
+    wt[16] = decay(X)
+    wt[17] = once
+    wt[18] = coef_rows * once
+    wt[19] = gain_rows
+
+    pl.semaphore_wait(barrier, nseq)
+    send_halo(0, 1)
     loads[4].wait()
     loads[5].wait()
     for ch in every:
-        phase_a(ch)
-    pl.semaphore_wait(barrier, nseq)
-    for ch in every:
+        phase_b(ch)
         start_z(z_b, zb_ss, zb_rs, ch, -1)
-    send_halo(0)
     loads[6].wait()
     f_s[...] = filt[...].astype(F32)
     for ch in every:
@@ -581,30 +579,36 @@
     phase_t(0)
     for ch in every:
         run_mid_b(ch)
-    for ch in range(1, CHUNKS):
-        send_halo(ch)
-    for ch in range(1, CHUNKS):
-        phase_t(ch)
+    send_halo(2, 3)
+    phase_t(1)
     loads[7].wait()
     loads[8].wait()
     run_u(0)
-    for ch in every:
-        run_bz(ch)
+    run_bz(0)
+    send_back(0, 1)
+    run_bz(1)
     phase_e(0)
     run_mid_s(0)
     phase_r(0)
-    for ch in range(1, CHUNKS):
-        run_u(ch)
-        phase_e(ch)
+    run_k(0)
+    phase_z(0)
+    run_u(1)
+    phase_e(1)
     phase_gf()
     for d in peers:
         scatter(d).start()
-    for ch in range(1, CHUNKS):
-        run_mid_s(ch)
-        phase_r(ch)
+    send_back(2)
+    rs[me] = part[me]
+    phase_r(1)
     phase_gr()
     swap_res.start()
-    rs[me] = part[me]
+    run_mid_s(1)
+    send_back(3)
+    phase_z(1)
+    swap_res.wait_recv()
+    res_all[me] = res[...] + res_dp[...]
+    for d in peers:
+        gather_res(d).start()
     for d in peers:
         scatter(d).wait_recv()
     own = rs[0]
@@ -612,25 +616,15 @@
         own = own + rs[i]
     dpx[0] = own
     swap.start()
-    for ch in every:
-        run_k(ch)
-    swap_res.wait_recv()
-    res_all[me] = res[...] + res_dp[...]
-    for d in peers:
-        gather_res(d).start()
+    run_d(0)
     swap.wait_recv()
     total[me] = dpx[0] + dpx[1]
     for d in peers:
         gather(d).start()
-    for ch in every:
-        phase_z(ch)
-    for ch in every:
-        run_d(ch)
-    for ch in every:
-        run_sz(ch)
-    for d in peers:
-        gather(d).wait_recv()
-    gf_o[...] = total[...].reshape(nb * G, L)
+    run_sz(0)
+    run_k(1)
+    run_d(1)
+    run_sz(1)
     for d in peers:
         gather_res(d).wait_recv()
     res_sum = res_all[0]
@@ -638,6 +632,9 @@
         res_sum = res_sum + res_all[i]
     wide = jnp.broadcast_to(res_sum[:, None, :], (nb, G, L)).reshape(nb * G, L)
     gr_o[...] = dot_exact(sel, jnp.where(spread, wide, 0.0), NT)
+    for d in peers:
+        gather(d).wait_recv()
+    gf_o[...] = total[...].reshape(nb * G, L)
 
     for i in range(CHUNKS * PIECES):
         @pl.when(me < nseq - 1)

time: 48.3 us -> 47.2 us (0.977)
  the two profiles are of different devices: /device:TPU:1 before, /device:TPU:6 now
where the time goes in v3:
time: 47.2 us; the launch traced here: 47.1 us
  Pallas kernels  46.4 us (98%)
  between operations  0.64 us (1%)
    pallas_call x1, Pallas kernels, per_device(): pl.pallas_call(functools.partial(kernel, nseq), out_shape=[big] * 5 + [ja...  44.9 us
    pallas_call x1, Pallas kernels, per_device(): pl.pallas_call(save_kernel, out_shape=[jax.ShapeDtypeStruct(o.shape, o.dt...  1.56 us

profile of v3, /device:TPU:6, one launch (start us, length us, event | category | flops | bytes accessed | tf_op | source)
XLA Modules:
  0.0 47.1 jit_solution(4669380419538101272)
XLA Ops:
  0.6 44.9 %hyena_bwd.1 = (bf16[2048,128]{1,0:T(8,128)(2,1)S(1)}, bf16[2048,128]{1,0:T(8,128)(2,1)S(1)}, bf16[2048,128]{1,0:T(8,128)(2,1)S(1)}, bf16[2048,128]{1,0:T(8,128)...) custom-call(bf16[2048,128]{1,0:T(8,128)(2,1)} %bitcast.14, ...), custom_call_target="tpu_custom_call" | custom-call | tf_op jit(solution)/shard_map/hyena_bwd/pallas_call | solution.py:690
  45.5 1.6 %hyena_save.1 = (bf16[2048,128]{1,0:T(8,128)(2,1)}, bf16[2048,128]{1,0:T(8,128)(2,1)}, bf16[2048,128]{1,0:T(8,128)(2,1)}, bf16[2048,128]{1,0:T(8,128)(2,1)}, bf1...) custom-call(bf16[2048,128]{1,0:T(8,128)(2,1)S(1)} %get-tuple-element.21.refs_0_, ...), custom_call_target="tpu_custom_call" | custom-call | tf_op jit(solution)/shard_map/hyena_save/pallas_call | solution.py:739

commit v4 on v3

--- a/solution.py
+++ b/solution.py
@@ -592,12 +592,12 @@
     phase_r(0)
     run_k(0)
     phase_z(0)
+    send_back(2)
     run_u(1)
     phase_e(1)
     phase_gf()
     for d in peers:
         scatter(d).start()
-    send_back(2)
     rs[me] = part[me]
     phase_r(1)
     phase_gr()

time: 47.2 us -> 45.8 us (0.970)
  the two profiles are of different devices: /device:TPU:6 before, /device:TPU:1 now
where the time goes in v4:
time: 45.8 us; the launch traced here: 45.3 us
  Pallas kernels  44.7 us (98%)
  between operations  0.64 us (1%)
    pallas_call x1, Pallas kernels, per_device(): pl.pallas_call(functools.partial(kernel, nseq), out_shape=[big] * 5 + [ja...  43.1 us
    pallas_call x1, Pallas kernels, per_device(): pl.pallas_call(save_kernel, out_shape=[jax.ShapeDtypeStruct(o.shape, o.dt...  1.56 us

profile of v4, /device:TPU:1, one launch (start us, length us, event | category | flops | bytes accessed | tf_op | source)
XLA Modules:
  0.0 45.3 jit_solution(9448602796206968592)
XLA Ops:
  0.6 43.1 %hyena_bwd.1 = (bf16[2048,128]{1,0:T(8,128)(2,1)S(1)}, bf16[2048,128]{1,0:T(8,128)(2,1)S(1)}, bf16[2048,128]{1,0:T(8,128)(2,1)S(1)}, bf16[2048,128]{1,0:T(8,128)...) custom-call(bf16[2048,128]{1,0:T(8,128)(2,1)} %bitcast.14, ...), custom_call_target="tpu_custom_call" | custom-call | tf_op jit(solution)/shard_map/hyena_bwd/pallas_call | solution.py:690
  43.8 1.6 %hyena_save.1 = (bf16[2048,128]{1,0:T(8,128)(2,1)}, bf16[2048,128]{1,0:T(8,128)(2,1)}, bf16[2048,128]{1,0:T(8,128)(2,1)}, bf16[2048,128]{1,0:T(8,128)(2,1)}, bf1...) custom-call(bf16[2048,128]{1,0:T(8,128)(2,1)S(1)} %get-tuple-element.21.refs_0_, ...), custom_call_target="tpu_custom_call" | custom-call | tf_op jit(solution)/shard_map/hyena_save/pallas_call | solution.py:739

commit v5 on v4

--- a/solution.py
+++ b/solution.py
@@ -599,11 +599,11 @@
     for d in peers:
         scatter(d).start()
     rs[me] = part[me]
+    send_back(3)
     phase_r(1)
     phase_gr()
     swap_res.start()
     run_mid_s(1)
-    send_back(3)
     phase_z(1)
     swap_res.wait_recv()
     res_all[me] = res[...] + res_dp[...]

time: 45.8 us -> 45.5 us (level)
  no operation moved by 1% of the time
where the time goes in v5:
time: 45.5 us; the launch traced here: 45.4 us
  Pallas kernels  44.7 us (98%)
  between operations  0.64 us (1%)
    pallas_call x1, Pallas kernels, per_device(): pl.pallas_call(functools.partial(kernel, nseq), out_shape=[big] * 5 + [ja...  43.2 us
    pallas_call x1, Pallas kernels, per_device(): pl.pallas_call(save_kernel, out_shape=[jax.ShapeDtypeStruct(o.shape, o.dt...  1.56 us

profile of v5, /device:TPU:1, one launch (start us, length us, event | category | flops | bytes accessed | tf_op | source)
XLA Modules:
  0.0 45.4 jit_solution(2503998066597432015)
XLA Ops:
  0.6 43.2 %hyena_bwd.1 = (bf16[2048,128]{1,0:T(8,128)(2,1)S(1)}, bf16[2048,128]{1,0:T(8,128)(2,1)S(1)}, bf16[2048,128]{1,0:T(8,128)(2,1)S(1)}, bf16[2048,128]{1,0:T(8,128)...) custom-call(bf16[2048,128]{1,0:T(8,128)(2,1)} %bitcast.14, ...), custom_call_target="tpu_custom_call" | custom-call | tf_op jit(solution)/shard_map/hyena_bwd/pallas_call | solution.py:690
  43.8 1.6 %hyena_save.1 = (bf16[2048,128]{1,0:T(8,128)(2,1)}, bf16[2048,128]{1,0:T(8,128)(2,1)}, bf16[2048,128]{1,0:T(8,128)(2,1)}, bf16[2048,128]{1,0:T(8,128)(2,1)}, bf1...) custom-call(bf16[2048,128]{1,0:T(8,128)(2,1)S(1)} %get-tuple-element.21.refs_0_, ...), custom_call_target="tpu_custom_call" | custom-call | tf_op jit(solution)/shard_map/hyena_save/pallas_call | solution.py:739
